TPU v7x, 256 devices: a whole 4x4x8 slice. The times are simulated.
256 devices in a mesh: op: 8 (over x, y_lo), str: 32 (over z, y_hi, core).
Axes of the slice: x: 4, y: 4 (y_hi: 2, y_lo: 2; y = y_hi * 2 + y_lo), z: 8, core: 2. Of those that a mesh axis runs over, the one named last changes fastest.
Arguments:
- coeffs: float32 [4096, 4096], P('str'), may hold values from -6 to 6
- previous: float32 [4096, 4096], P('str'), may hold values from -6 to 6
- block_values: bfloat16 [8, 32, 6, 128, 128], P('op'), may hold values from -0.21875 to 0.21875
- block_cols: int32 [8, 32, 6], P('op'), may hold values from 0 to 31, as said below
Outputs:
- advanced: float32 [4096, 4096], P('str')
Inputs may be any that keep to these rules, and one draw needn't show every extreme that they name: For every term k and block row r, block_cols[k, r, 0] equals r and the 6 entries of block_cols[k, r] are distinct.
All inputs are finite; a program needn't handle non-finite values.
Results may differ from a plain program's by a relative error of at most 0.0003.
Values sent between devices are 32-bit elements; how exact they have to be, the bound alone decides.
No kernel may reach another device: no remote copies, remote signals or barrier semaphores. Data moves between devices by JAX's collectives and lax.ppermute only.
A program may use at most 128 MiB of HBM per device.

v0:
```python
import math

import jax
import jax.numpy as jnp
from jax import lax
from jax.sharding import Mesh
from jax.sharding import PartitionSpec as P

STEPS = 2
STR = ("str_0", "str_1", "str_2")


def split_up(array, dim, size):
    dims = array.shape
    blocks = array.reshape(*dims[:dim], size, dims[dim] // size, *dims[dim + 1 :])
    return jnp.moveaxis(blocks, dim, 0)


def laid_out(blocks, dim):
    blocks = jnp.moveaxis(blocks, 0, dim)
    dims = blocks.shape
    return blocks.reshape(*dims[:dim], dims[dim] * dims[dim + 1], *dims[dim + 2 :])


def exchange_in_order(blocks, axes, sequence):
    inside = blocks.shape[1:]
    out = blocks.reshape(*(lax.axis_size(a) for a in axes), *inside)
    for k in sequence:
        out = lax.all_to_all(out, axes[k], k, k, tiled=True)
    return out.reshape(-1, *inside)


def core_and_chips(array, groups, sequence, split_dim, concat_dim):
    size = lax.axis_size(groups[0]) * lax.axis_size(groups[1])
    blocks = split_up(array, split_dim, size)
    return laid_out(exchange_in_order(blocks, groups, sequence), concat_dim)


def per_device(coeffs, previous, block_values, block_cols):
    local_terms = block_values.shape[0]
    step_scale = 2.0 / math.sqrt(local_terms * lax.axis_size("op"))
    factors = block_values.astype(jnp.float32)
    row_count, full_width = coeffs.shape
    block_size = block_values.shape[-1]
    block_count = full_width // block_size
    slot_count = block_cols.shape[2]
    regrouped = core_and_chips(
        previous.reshape(row_count, block_count, block_size),
        (("str_0", "str_1"), "str_2"),
        (1, 0),
        1,
        0,
    )
    earlier = regrouped.reshape(full_width, row_count).T
    current = coeffs
    for step_index in range(STEPS):
        column_list = block_cols[0].reshape(-1)
        term_factors = factors[0]
        gathered = jnp.take(
            current.reshape(row_count, block_count, block_size), column_list, axis=1
        )
        gathered = gathered.reshape(row_count, block_count, slot_count, block_size)
        beta_side = jnp.einsum(
            "arjc,rjoc->aro", gathered, term_factors, precision=lax.Precision.HIGHEST
        )
        received = lax.all_to_all(beta_side, STR, split_axis=1, concat_axis=0, tiled=True)
        group_count = received.shape[1]
        item_count = received.shape[2]
        grouped = jnp.take(
            received.reshape(block_count, block_size, group_count, item_count), column_list, axis=0
        )
        grouped = grouped.reshape(block_count, slot_count, block_size, group_count, item_count)
        result = jnp.einsum(
            "rjoc,rjcnm->nmro", term_factors, grouped, precision=lax.Precision.HIGHEST
        )
        moved = result.reshape(group_count, item_count, full_width)
        summed = moved.reshape(row_count, full_width)
        updated = step_scale * lax.psum(summed, "op") - earlier
        earlier, current = (current, updated)
    return current


def solution(mesh):
    torus = Mesh(mesh.devices.reshape(mesh.shape["op"], 8, 2, 2), ("op", "str_0", "str_1", "str_2"))
    placed = (P(STR, None), P(STR, None), P("op", None, None, None, None), P("op", None, None))
    return jax.shard_map(
        per_device, mesh=torus, in_specs=placed, out_specs=P(STR, None), check_vma=False
    )
```

profile of v0, /device:TPU:16, one launch (start us, length us, event | category | flops | bytes accessed | tf_op | source)
XLA Modules:
  0.0 504.8 jit_solution(10311836481137910185)
XLA Ops:
  6.5 1.9 copy.39
  8.5 1.8 copy.41
  10.3 4.9 all-to-all-start.1
  15.3 0.1 reshape_squeeze.4
  15.4 2.9 copy.37
  18.3 1.9 copy.38
  20.2 5.9 %gather_fusion = f32[192,128,128]{2,1,0:T(8,128)} fusion(f32[128,32,128]{2,0,1:T(8,128)S(1)} %copy.38, s32[1024]{0:T(1024)S(1)} %pad_clamp_fusion), kind=kCustom, calls=%fused_computation.clone | custom fusion | bytes 25166592 | tf_op jit(solution)/shard_map/jit(_take)/gather | solution.py:59
  26.1 10.0 %broadcast_select_fusion.1 = f32[192,128,128]{2,1,0:T(8,128)} fusion(f32[192,128,128]{2,1,0:T(8,128)} %gather_fusion, pred[192]{0:T(512)(128)(4,1)S(1)} %compare_and_fusion), kind=kLoop, calls=%fused_computation.15 | loop fusion | flops 3145728 | bytes 25166016 | tf_op jit(solution)/shard_map/jit(_take)/select_n | solution.py:59
  36.1 13.3 %fusion.8 = f32[128,32,128]{2,0,1:T(8,128)} fusion(f32[128,32,6,128]{3,0,2,1:T(8,128)} %bitcast.77, bf16[1,32,6,128,128]{4,3,2,1,0:T(8,128)(2,1)} %param.10), kind=kOutput, calls=%fused_computation.18 | convolution fusion | flops 4831838208 | bytes 20971520 | tf_op jit(solution)/shard_map/arjc,rjoc->aro/dot_general | solution.py:63
  49.4 11.7 %all-to-all-start = ((f32[128,32,128]{2,0,1:T(8,128)}), f32[128,32,128]{2,0,1:T(8,128)S(1)}, u32[]{:S(2)}, u32[]{:S(2)}) async-start(f32[128,32,128]{2,0,1:T(8,128)} %fusion.8), calls=%async_computation | async-start | bytes 4194304 | tf_op jit(solution)/shard_map/all_to_all | solution.py:66
  61.1 3.1 copy.42
  64.2 47.1 %all-to-all-done = f32[128,32,128]{2,0,1:T(8,128)S(1)} async-done(((f32[128,32,128]{2,0,1:T(8,128)}), f32[128,32,128]{2,0,1:T(8,128)S(1)}, u32[]{:S(2)}, u32[]{:S(2)}) %all-to-all-start) | async-done | bytes 2097184 | tf_op jit(solution)/shard_map/all_to_all | solution.py:66
  111.3 6.0 %all-to-all-start.2 = ((f32[16,2,128,1,128]{4,2,1,3,0:T(8,128)}), f32[16,2,128,1,128]{4,2,1,3,0:T(8,128)}, u32[]{:S(2)}, u32[]{:S(2)}) async-start(f32[16,2,128,1,128]{4,2,1,3,0:T(8,128)} %copy.42), calls=%async_computation.2 | async-start | bytes 4194304 | tf_op jit(solution)/shard_map/all_to_all | solution.py:29
  117.4 0.5 all-reduce.3.cloned.1.call-start
  117.9 5.9 %gather_fusion.1 = f32[192,128,128]{2,1,0:T(8,128)} fusion(f32[32,128,128]{2,1,0:T(8,128)S(1)} %bitcast.74, s32[1024]{0:T(1024)S(1)} %pad_clamp_fusion), kind=kCustom, calls=%fused_computation.1.clone | custom fusion | bytes 25166592 | tf_op jit(solution)/shard_map/jit(_take)/gather | solution.py:69
  123.8 10.0 %bitcast_select_fusion.1 = f32[192,128,1,128]{3,1,0,2:T(8,128)} fusion(f32[192,128,128]{2,1,0:T(8,128)} %gather_fusion.1, pred[192]{0:T(512)(128)(4,1)S(1)} %compare_and_fusion), kind=kLoop, calls=%fused_computation.5 | loop fusion | flops 3145728 | bytes 25166016 | tf_op jit(solution)/shard_map/jit(_take)/select_n | solution.py:69
  133.8 14.7 %fusion.4 = f32[32,128,128,1]{1,2,3,0:T(8,128)} fusion(f32[32,6,128,128]{3,2,1,0:T(8,128)} %bitcast.78, bf16[1,32,6,128,128]{4,3,2,1,0:T(8,128)(2,1)} %param.10), kind=kOutput, calls=%fused_computation.10 | convolution fusion | flops 4831838208 | bytes 20971520 | tf_op jit(solution)/shard_map/rjoc,rjcnm->nmro/dot_general | solution.py:73
  148.5 0.2 all-reduce.5.cloned.1.call-start
  148.7 19.7 %all-to-all-done.2 = f32[16,2,128,1,128]{4,2,1,3,0:T(8,128)} async-done(((f32[16,2,128,1,128]{4,2,1,3,0:T(8,128)}), f32[16,2,128,1,128]{4,2,1,3,0:T(8,128)}, u32[]{:S(2)}, u32[]{:S(2)}) %all-to-all-start.2) | async-done | bytes 2097184 | tf_op jit(solution)/shard_map/all_to_all | solution.py:29
  168.4 91.6 %all-reduce.3.cloned.1.call-done = f32[128,4096]{0,1:T(8,128)} async-done(((f32[128,4096]{0,1:T(8,128)}), f32[128,4096]{0,1:T(8,128)}) %all-reduce.3.cloned.1.call-update) | async-done | bytes 2097168 | tf_op jit(solution)/shard_map/psum | solution.py:78
  260.0 3.8 bitcast_subtract_fusion
  263.8 1.9 copy.43
  265.7 5.9 %gather_fusion.2 = f32[192,128,128]{2,1,0:T(8,128)} fusion(f32[128,32,128]{2,0,1:T(8,128)S(1)} %copy.43, s32[1024]{0:T(1024)S(1)} %pad_clamp_fusion), kind=kCustom, calls=%fused_computation.2.clone | custom fusion | bytes 25166592 | tf_op jit(solution)/shard_map/jit(_take)/gather | solution.py:59
  271.6 10.0 %broadcast_select_fusion = f32[192,128,128]{2,1,0:T(8,128)} fusion(f32[192,128,128]{2,1,0:T(8,128)} %gather_fusion.2, pred[192]{0:T(512)(128)(4,1)S(1)} %compare_and_fusion), kind=kLoop, calls=%fused_computation.14 | loop fusion | flops 3145728 | bytes 25166016 | tf_op jit(solution)/shard_map/jit(_take)/select_n | solution.py:59
  281.6 13.3 %fusion.11 = f32[128,32,128]{2,0,1:T(8,128)} fusion(f32[128,32,6,128]{3,0,2,1:T(8,128)} %bitcast.79, bf16[1,32,6,128,128]{4,3,2,1,0:T(8,128)(2,1)} %param.10), kind=kOutput, calls=%fused_computation.19 | convolution fusion | flops 4831838208 | bytes 20971520 | tf_op jit(solution)/shard_map/arjc,rjoc->aro/dot_general | solution.py:63
  294.9 61.8 %all_to_all.40 = f32[128,32,128]{2,0,1:T(8,128)S(1)} all-to-all(f32[128,32,128]{2,0,1:T(8,128)} %fusion.11), channel_id=1, replica_groups=mesh['op'=8,'str_0'=8,'str_1'=2,'str_2'=2] {'str_0','str_1','str_2'}, dimensions={1} | all-to-all | bytes 4194304 | tf_op jit(solution)/shard_map/all_to_all | solution.py:66
  356.6 5.9 %gather_fusion.3 = f32[192,128,128]{2,1,0:T(8,128)} fusion(f32[32,128,128]{2,1,0:T(8,128)S(1)} %bitcast.75, s32[1024]{0:T(1024)S(1)} %pad_clamp_fusion), kind=kCustom, calls=%fused_computation.3.clone | custom fusion | bytes 25166592 | tf_op jit(solution)/shard_map/jit(_take)/gather | solution.py:69
  362.5 10.0 %bitcast_select_fusion = f32[192,128,1,128]{3,1,0,2:T(8,128)} fusion(f32[192,128,128]{2,1,0:T(8,128)} %gather_fusion.3, pred[192]{0:T(512)(128)(4,1)S(1)} %compare_and_fusion), kind=kLoop, calls=%fused_computation.4 | loop fusion | flops 3145728 | bytes 25166016 | tf_op jit(solution)/shard_map/jit(_take)/select_n | solution.py:69
  372.5 14.8 %fusion = f32[32,128,128,1]{1,2,3,0:T(8,128)} fusion(f32[32,6,128,128]{3,2,1,0:T(8,128)} %bitcast.76, bf16[1,32,6,128,128]{4,3,2,1,0:T(8,128)(2,1)} %param.10), kind=kOutput, calls=%fused_computation.6 | convolution fusion | flops 4831838208 | bytes 20971520 | tf_op jit(solution)/shard_map/rjoc,rjcnm->nmro/dot_general | solution.py:73
  387.3 104.4 %all-reduce.5.cloned.1.call-done = f32[128,4096]{0,1:T(8,128)} async-done(((f32[128,4096]{0,1:T(8,128)}), f32[128,4096]{0,1:T(8,128)}) %all-reduce.5.cloned.1.call-update) | async-done | bytes 2097168 | tf_op jit(solution)/shard_map/psum | solution.py:78
  491.7 3.1 multiply_subtract_fusion
  494.9 2.9 copy.45
  (11 shorter events, 0.1 us)
Async XLA Ops:
  6.5 8.6 %copy-start.1 = (s32[1,32,6]{1,0,2:T(1,128)S(1)}, s32[1,32,6]{1,0,2:T(1,128)}, u32[]{:S(2)}) copy-start(s32[1,32,6]{1,0,2:T(1,128)} %param.11) | copy-start | bytes 2308
  10.3 39.1 %all-to-all-start.1 = ((f32[16,2,128,1,128]{4,2,0,3,1:T(8,128)}), f32[16,2,128,1,128]{4,2,0,3,1:T(8,128)}, u32[]{:S(2)}, u32[]{:S(2)}) async-start(f32[16,2,128,1,128]{4,2,0,3,1:T(8,128)} %copy.41), calls=%async_computation.1 | async-start | bytes 4194304 | tf_op jit(solution)/shard_map/all_to_all | solution.py:29
  49.4 61.9 %all-to-all-start = ((f32[128,32,128]{2,0,1:T(8,128)}), f32[128,32,128]{2,0,1:T(8,128)S(1)}, u32[]{:S(2)}, u32[]{:S(2)}) async-start(f32[128,32,128]{2,0,1:T(8,128)} %fusion.8), calls=%async_computation | async-start | bytes 4194304 | tf_op jit(solution)/shard_map/all_to_all | solution.py:66
  111.3 57.1 %all-to-all-start.2 = ((f32[16,2,128,1,128]{4,2,1,3,0:T(8,128)}), f32[16,2,128,1,128]{4,2,1,3,0:T(8,128)}, u32[]{:S(2)}, u32[]{:S(2)}) async-start(f32[16,2,128,1,128]{4,2,1,3,0:T(8,128)} %copy.42), calls=%async_computation.2 | async-start | bytes 4194304 | tf_op jit(solution)/shard_map/all_to_all | solution.py:29
  117.4 142.6 %all-reduce.3.cloned.1.call-start = ((), (), s32[]{:S(2)}) async-start(), calls=%async_computation.4 | async-start | bytes 4194304 | tf_op jit(solution)/shard_map/psum | solution.py:78
  148.5 343.3 %all-reduce.5.cloned.1.call-start = ((), (), s32[]{:S(2)}) async-start(), calls=%async_computation.5 | async-start | bytes 4194304 | tf_op jit(solution)/shard_map/psum | solution.py:78
  372.5 119.2 %copy-start = (f32[128,4096]{0,1:T(8,128)S(1)}, f32[128,4096]{0,1:T(8,128)}, u32[]{:S(2)}) copy-start(f32[128,4096]{0,1:T(8,128)} %copy.37) | copy-start | bytes 6291460
Sparse Core Ops, SparseCore 0:
  148.6 111.3 all-reduce.2
  387.4 104.2 all-reduce.4
where the time goes:
time: 513 us; the launch traced here: 505 us
  waiting for transfers between devices  263 us (51%)
  blocking collectives  61.8 us (12%)
  matrix products  56 us (11%)
  other arithmetic  47 us (9%)
  local copies, waits for them, and re-layouts  40.2 us (8%)
  starting transfers between devices  23.3 us (5%)
  between operations  13.7 us (3%)
    psum x2, waiting for transfers between devices, per_device(): updated = step_scale * lax.psum(summed, 'op') - earlier  196 us
    all_to_all x1, blocking collectives, per_device(): lax.all_to_all(beta_side, STR, split_axis=1, concat_axis=0, tiled=True)  61.8 us
    all_to_all x1, waiting for transfers between devices, per_device(): lax.all_to_all(beta_side, STR, split_axis=1, concat_axis=0, tiled=True)  47.1 us
    dot_general x2, matrix products, per_device(): jnp.einsum('rjoc,rjcnm->nmro', term_factors, grouped, precision=lax.Preci...  29.4 us
    dot_general x2, matrix products, per_device(): jnp.einsum('arjc,rjoc->aro', gathered, term_factors, precision=lax.Precis...  26.6 us
    select_n x3, other arithmetic, per_device(): jnp.take(received.reshape(block_count, block_size, group_count, item_coun...  20 us
    select_n x2, other arithmetic, per_device(): jnp.take(current.reshape(row_count, block_count, block_size), column_list...  20 us
    all_to_all x2, waiting for transfers between devices, exchange_in_order(): out = lax.all_to_all(out, axes[k], k, k, tiled=True)  19.7 us
  transfers between devices with their start and end apart: 5, of which 4 were waited for; matrix products, arithmetic and copies ran while one was open for 13% of the time, Pallas kernels for 0%

commit v1 on v0

v1 whole, which is shorter than its diff:
```python
import functools
import math

import jax
import jax.numpy as jnp
from jax import lax
from jax.experimental import pallas as pl
from jax.experimental.pallas import tpu as pltpu
from jax.sharding import PartitionSpec as P

BLOCK = 128
CHUNKS = 2
ROWS_PER_STEP = 8


def split(values):
    high = values.astype(jnp.bfloat16)
    return high, (values - high.astype(jnp.float32)).astype(jnp.bfloat16)


def side_kernel(cols, *refs, blocked_in, turned_in, turned_out, rows, slots, per_step):
    field_count = len(turned_in) if turned_in else 1
    fields, factors, outs, halves = refs[:field_count], refs[field_count], refs[field_count + 1 : -1], refs[-1]
    step = pl.program_id(0)
    count = halves.shape[0]

    @pl.when(step == 0)
    def _():
        def prepare(c, carry):
            if turned_in:
                block = jnp.concatenate([f[c] for f in fields], axis=0).T
            elif blocked_in:
                block = fields[0][c]
            else:
                block = fields[0][:, pl.ds(pl.multiple_of(c * BLOCK, BLOCK), BLOCK)]
            high, low = split(block)
            halves[c, :rows] = high
            halves[c, rows:] = low
            return carry

        lax.fori_loop(0, count, prepare, 0, unroll=4)

    for i in range(per_step):
        base = (step * per_step + i) * slots
        gathered = jnp.concatenate([halves[cols[base + j]] for j in range(slots)], axis=1)
        factor = jnp.concatenate([factors[i, j] for j in range(slots)], axis=1)
        if turned_out:
            both = lax.dot_general(
                factor, gathered, (((1,), (1,)), ((), ())), preferred_element_type=jnp.float32
            )
            total = both[:, :rows] + both[:, rows:]
            size = BLOCK // len(outs)
            for q, out in enumerate(outs):
                out[i] = total[q * size : (q + 1) * size]
        else:
            both = lax.dot_general(
                gathered, factor, (((1,), (1,)), ((), ())), preferred_element_type=jnp.float32
            )
            total = both[:rows] + both[rows:]
            if len(outs[0].shape) == 3:
                outs[0][i] = total
            else:
                outs[0][:, i * BLOCK : (i + 1) * BLOCK] = total


def side(cols, fields, factors, form):
    blocks, slots = factors.shape[:2]
    per_step = ROWS_PER_STEP
    turned_in = tuple(fields) if form == "alpha_turned" else ()
    blocked_in = form == "alpha"
    if turned_in:
        rows = fields[0].shape[2]
    else:
        rows = fields[0].shape[1 if blocked_in else 0]
    if form == "beta_turned":
        size = BLOCK // CHUNKS
        out_shape = [jax.ShapeDtypeStruct((blocks, size, rows), jnp.float32)] * CHUNKS
        out_specs = [pl.BlockSpec((per_step, size, rows), lambda i, c: (i, 0, 0))] * CHUNKS
    elif form == "beta":
        out_shape = [jax.ShapeDtypeStruct((blocks, rows, BLOCK), jnp.float32)]
        out_specs = [pl.BlockSpec((per_step, rows, BLOCK), lambda i, c: (i, 0, 0))]
    else:
        out_shape = [jax.ShapeDtypeStruct((rows, blocks * BLOCK), jnp.float32)]
        out_specs = [pl.BlockSpec((rows, per_step * BLOCK), lambda i, c: (0, i))]
    in_specs = [
        pl.BlockSpec(f.shape, (lambda i, c: (0, 0, 0)) if len(f.shape) == 3 else (lambda i, c: (0, 0)))
        for f in fields
    ]
    in_specs.append(pl.BlockSpec((per_step, slots, BLOCK, BLOCK), lambda i, c: (i, 0, 0, 0)))
    return pl.pallas_call(
        functools.partial(
            side_kernel,
            blocked_in=blocked_in,
            turned_in=turned_in,
            turned_out=form == "beta_turned",
            rows=rows,
            slots=slots,
            per_step=per_step,
        ),
        out_shape=out_shape,
        grid_spec=pltpu.PrefetchScalarGridSpec(
            num_scalar_prefetch=1,
            grid=(blocks // per_step,),
            in_specs=in_specs,
            out_specs=out_specs,
            scratch_shapes=[pltpu.VMEM((blocks, 2 * rows, BLOCK), jnp.bfloat16)],
        ),
        compiler_params=pltpu.CompilerParams(vmem_limit_bytes=40 << 20),
        cost_estimate=pl.CostEstimate(
            flops=4 * rows * blocks * slots * BLOCK * BLOCK,
            bytes_accessed=factors.size * 2 + 8 * rows * blocks * BLOCK,
            transcendentals=0,
        ),
        name=form,
    )(cols, *fields, factors)


def turn_kernel(place, field, out, scratch):
    blocks, chunks, size = out.shape[:3]
    me = place[0]

    def one(c, carry):
        scratch[...] = field[:, pl.ds(pl.multiple_of(c * BLOCK, BLOCK), BLOCK)].T
        for q in range(chunks):
            start = pl.multiple_of(q * (BLOCK // chunks) + me * size, 8)
            out[c, q] = scratch[pl.ds(start, size)]
        return carry

    lax.fori_loop(0, blocks, one, 0, unroll=4)


def turned_share(field, shares):
    blocks = field.shape[1] // BLOCK
    size = BLOCK // CHUNKS // shares
    place = lax.axis_index("op").astype(jnp.int32).reshape(1)
    return pl.pallas_call(
        turn_kernel,
        out_shape=jax.ShapeDtypeStruct((blocks, CHUNKS, size, BLOCK), jnp.float32),
        in_specs=[
            pl.BlockSpec(memory_space=pltpu.SMEM),
            pl.BlockSpec(memory_space=pltpu.VMEM),
        ],
        out_specs=pl.BlockSpec(memory_space=pltpu.VMEM),
        scratch_shapes=[pltpu.VMEM((BLOCK, BLOCK), jnp.float32)],
        compiler_params=pltpu.CompilerParams(vmem_limit_bytes=40 << 20),
        name="turn",
    )(place, field)


def exchange(blocks, axis):
    return lax.all_to_all(blocks, axis, 0, 0, tiled=True)


def shared(part, shares):
    copies = jnp.broadcast_to(part[None], (shares, *part.shape))
    return exchange(copies, "op").reshape(-1, part.shape[-1])


def per_device(coeffs, previous, block_values, block_cols):
    shares = lax.axis_size("op")
    step_scale = 2.0 / math.sqrt(block_values.shape[0] * shares)
    width = coeffs.shape[1]
    factors = block_values[0]
    cols = block_cols[0].reshape(-1)
    me = lax.axis_index("op")

    def summed(partial):
        received = exchange(partial, "op").reshape(shares, -1, width)
        return jnp.sum(received, axis=0)

    parts = side(cols, [coeffs], factors, "beta_turned")
    before = exchange(turned_share(previous, shares), "str")
    sent = []
    for q in range(CHUNKS):
        (result,) = side(cols, [exchange(parts[q], "str")], factors, "alpha")
        earlier = before[:, q].transpose(1, 0, 2).reshape(-1, width)
        current = shared(step_scale * summed(result) - earlier, shares)
        (beta,) = side(cols, [current], factors, "beta")
        sent.append(exchange(beta, "str"))
    (result,) = side(cols, sent, factors, "alpha_turned")
    rows = coeffs.shape[0] // shares
    earlier = lax.dynamic_slice_in_dim(coeffs, me * rows, rows, 0)
    return shared(step_scale * summed(result) - earlier, shares)


def solution(mesh):
    placed = (P("str", None), P("str", None), P("op", None, None, None, None), P("op", None, None))
    return jax.shard_map(
        per_device, mesh=mesh, in_specs=placed, out_specs=P("str", None), check_vma=False
    )
```

time: 513 us -> 326 us (0.64); the launches traced: 505 us -> 325 us
  waiting for transfers between devices: 263 us -> 115 us
  blocking collectives: 61.8 us -> 120 us
  matrix products: 56 us -> 0 us
  other arithmetic: 47 us -> 2.49 us
  Pallas kernels: 0 us -> 29.4 us
  local copies, waits for them, and re-layouts: 40.2 us -> 21.8 us
  between operations: 13.7 us -> 0.16 us
  starting transfers between devices: 23.3 us -> 36 us
    psum x2 -> x0, waiting for transfers between devices: 196 us -> none  [per_device(): updated = step_scale * lax.psum(summed, 'op') - earlier]
    all_to_all x1 -> x4, blocking collectives: 61.8 us -> 120 us  [exchange(): return lax.all_to_all(blocks, axis, 0, 0, tiled=True)]
    dot_general x4 -> x0, matrix products: 56 us -> none  [the longest x2 29.4 us: per_device(): jnp.einsum('rjoc,rjcnm->nmro', term_factors, grouped, precision=lax.Preci...]
    all_to_all x3 -> x7, waiting for transfers between devices: 66.8 us -> 115 us  [exchange(): return lax.all_to_all(blocks, axis, 0, 0, tiled=True)]
    select_n x5 -> x0, other arithmetic: 40.1 us -> none  [the longest x3 20 us: per_device(): jnp.take(received.reshape(block_count, block_size, group_count, item_coun...]
    pallas_call x0 -> x7, Pallas kernels: none -> 29.4 us  [the longest x6 27.6 us: side(): pl.pallas_call(functools.partial(side_kernel, blocked_in=blocked_in, turn...]
    gather x4 -> x0, local copies, waits for them, and re-layouts: 23.6 us -> none  [the longest x2 11.8 us: per_device(): jnp.take(current.reshape(row_count, block_count, block_size), column_list...]
    unnamed x7 -> x18, local copies, waits for them, and re-layouts: 4.9 us -> 20.4 us
  transfers between devices with their start and end apart: 5 -> 7, of which waited for: 4 -> 7; matrix products, arithmetic and copies ran while one was open for 13% -> 0% of each run, Pallas kernels for 0% -> 5%
where the time goes in v1:
time: 326 us; the launch traced here: 325 us
  blocking collectives  120 us (37%)
  waiting for transfers between devices  115 us (35%)
  starting transfers between devices  36 us (11%)
  Pallas kernels  29.4 us (9%)
  local copies, waits for them, and re-layouts  21.8 us (7%)
    all_to_all x4, blocking collectives, exchange(): return lax.all_to_all(blocks, axis, 0, 0, tiled=True)  120 us
    all_to_all x7, waiting for transfers between devices, exchange(): return lax.all_to_all(blocks, axis, 0, 0, tiled=True)  115 us
    all_to_all x7, starting transfers between devices, exchange(): return lax.all_to_all(blocks, axis, 0, 0, tiled=True)  36 us
    pallas_call x6, Pallas kernels, side(): pl.pallas_call(functools.partial(side_kernel, blocked_in=blocked_in, turn...  27.6 us
    unnamed x18, local copies, waits for them, and re-layouts  20.4 us
  transfers between devices with their start and end apart: 7, of which 7 were waited for; matrix products, arithmetic and copies ran while one was open for 0% of the time, Pallas kernels for 5%

profile of v1, /device:TPU:16, one launch (start us, length us, event | category | flops | bytes accessed | tf_op | source)
XLA Modules:
  0.0 325.4 jit_solution(14760180105586838369)
XLA Ops:
  0.9 2.8 copy-done
  3.7 1.6 copy-done.6
  5.2 6.3 %beta_turned.1 = (f32[32,64,128]{2,1,0:T(8,128)S(1)}, f32[32,64,128]{2,1,0:T(8,128)}) custom-call(s32[192]{0:T(256)S(1)} %reshape_squeeze.3.cols, f32[128,4096]{1,0:T(8,128)S(1)} %copy-done.6, bf16[32,6,128,128]{3,2,1,0:T(8,128)(2,1)S(1)} %bitcast.24), custom_call_target="tpu_custom_call" | custom-call | flops 1610612736 | bytes 10485760 | tf_op jit(solution)/shard_map/beta_turned/pallas_call | solution.py:90
  11.5 40.3 %all_to_all.67.refs_0_ = f32[32,64,128]{2,1,0:T(8,128)S(1)} all-to-all(f32[32,64,128]{2,1,0:T(8,128)S(1)} %get-tuple-element.7), channel_id=1, replica_groups=mesh['op'=8,'str'=32] {'str'}, dimensions={0} | all-to-all | bytes 2097152 | tf_op jit(solution)/shard_map/all_to_all | solution.py:151
  51.8 5.0 %all-to-all-start.5 = ((f32[32,64,128]{2,1,0:T(8,128)}), f32[32,64,128]{2,1,0:T(8,128)S(1)}, u32[]{:S(2)}, u32[]{:S(2)}) async-start(f32[32,64,128]{2,1,0:T(8,128)} %get-tuple-element.8), calls=%async_computation.5 | async-start | bytes 2097152 | tf_op jit(solution)/shard_map/all_to_all | solution.py:151
  56.8 2.8 copy-done.1
  59.6 3.9 %alpha.2 = f32[64,4096]{1,0:T(8,128)} custom-call(s32[192]{0:T(256)S(1)} %reshape_squeeze.3.cols, f32[32,64,128]{2,1,0:T(8,128)S(1)} %all_to_all.67.refs_0_, bf16[32,6,128,128]{3,2,1,0:T(8,128)(2,1)S(1)} %bitcast.25), custom_call_target="tpu_custom_call" | custom-call | flops 805306368 | bytes 8388608 | tf_op jit(solution)/shard_map/alpha/pallas_call | solution.py:90
  63.5 22.3 %all-to-all-done.5.refs_0_ = f32[32,64,128]{2,1,0:T(8,128)S(1)} async-done(((f32[32,64,128]{2,1,0:T(8,128)}), f32[32,64,128]{2,1,0:T(8,128)S(1)}, u32[]{:S(2)}, u32[]{:S(2)}) %all-to-all-start.5) | async-done | bytes 1048608 | tf_op jit(solution)/shard_map/all_to_all | solution.py:151
  85.8 5.0 %all-to-all-start.1 = ((f32[8,8,4096]{2,1,0:T(8,128)}), f32[8,8,4096]{2,1,0:T(8,128)S(1)}, u32[]{:S(2)}, u32[]{:S(2)}) async-start(f32[8,8,4096]{2,1,0:T(8,128)} %bitcast.1), calls=%async_computation.1 | async-start | bytes 2097152 | tf_op jit(solution)/shard_map/all_to_all | solution.py:151
  90.8 2.8 copy-done.2
  93.6 3.9 %alpha.3 = f32[64,4096]{1,0:T(8,128)} custom-call(s32[192]{0:T(256)S(1)} %reshape_squeeze.3.cols, f32[32,64,128]{2,1,0:T(8,128)S(1)} %all-to-all-done.5.refs_0_, bf16[32,6,128,128]{3,2,1,0:T(8,128)(2,1)S(1)} %bitcast.26), custom_call_target="tpu_custom_call" | custom-call | flops 805306368 | bytes 8388608 | tf_op jit(solution)/shard_map/alpha/pallas_call | solution.py:90
  97.5 8.5 %all-to-all-done.1 = f32[8,8,4096]{2,1,0:T(8,128)S(1)} async-done(((f32[8,8,4096]{2,1,0:T(8,128)}), f32[8,8,4096]{2,1,0:T(8,128)S(1)}, u32[]{:S(2)}, u32[]{:S(2)}) %all-to-all-start.1) | async-done | bytes 1048608 | tf_op jit(solution)/shard_map/all_to_all | solution.py:151
  106.0 4.3 %all-to-all-start.6 = ((f32[8,8,4096]{2,1,0:T(8,128)}), f32[8,8,4096]{2,1,0:T(8,128)}, u32[]{:S(2)}, u32[]{:S(2)}) async-start(f32[8,8,4096]{2,1,0:T(8,128)} %bitcast.7), calls=%async_computation.6 | async-start | bytes 2097152 | tf_op jit(solution)/shard_map/all_to_all | solution.py:151
  110.3 1.9 turn.1
  112.1 12.8 %all-to-all-done.6 = f32[8,8,4096]{2,1,0:T(8,128)} async-done(((f32[8,8,4096]{2,1,0:T(8,128)}), f32[8,8,4096]{2,1,0:T(8,128)}, u32[]{:S(2)}, u32[]{:S(2)}) %all-to-all-start.6) | async-done | bytes 1048608 | tf_op jit(solution)/shard_map/all_to_all | solution.py:151
  125.0 7.1 %all-to-all-start.2 = ((f32[32,2,8,128]{3,2,1,0:T(8,128)}), f32[32,2,8,128]{3,2,1,0:T(8,128)S(1)}, u32[]{:S(2)}, u32[]{:S(2)}) async-start(f32[32,2,8,128]{3,2,1,0:T(8,128)} %turn.1), calls=%async_computation.2 | async-start | bytes 524288 | tf_op jit(solution)/shard_map/all_to_all | solution.py:151
  133.5 10.7 %all-to-all-done.2 = f32[32,2,8,128]{3,2,1,0:T(8,128)S(1)} async-done(((f32[32,2,8,128]{3,2,1,0:T(8,128)}), f32[32,2,8,128]{3,2,1,0:T(8,128)S(1)}, u32[]{:S(2)}, u32[]{:S(2)}) %all-to-all-start.2) | async-done | bytes 262176 | tf_op jit(solution)/shard_map/all_to_all | solution.py:151
  144.3 17.9 %all_to_all.68 = f32[8,8,4096]{2,1,0:T(8,128)S(1)} all-to-all(f32[8,8,4096]{2,1,0:T(8,128)S(1)} %broadcast_in_dim.7), channel_id=1, replica_groups=mesh['op'=8,'str'=32] {'op'}, dimensions={0} | all-to-all | bytes 2097152 | tf_op jit(solution)/shard_map/all_to_all | solution.py:151
  163.2 3.6 %all-to-all-start.3 = ((f32[8,8,4096]{2,1,0:T(8,128)}), f32[8,8,4096]{2,1,0:T(8,128)S(1)}, u32[]{:S(2)}, u32[]{:S(2)}) async-start(f32[8,8,4096]{2,1,0:T(8,128)} %broadcast_in_dim.6), calls=%async_computation.3 | async-start | bytes 2097152 | tf_op jit(solution)/shard_map/all_to_all | solution.py:151
  166.8 2.8 copy-done.3
  169.6 3.9 %beta.3 = f32[32,64,128]{2,1,0:T(8,128)} custom-call(s32[192]{0:T(256)S(1)} %reshape_squeeze.3.cols, f32[64,4096]{1,0:T(8,128)S(1)} %bitcast.31, bf16[32,6,128,128]{3,2,1,0:T(8,128)(2,1)S(1)} %bitcast.27), custom_call_target="tpu_custom_call" | custom-call | flops 805306368 | bytes 8388608 | tf_op jit(solution)/shard_map/beta/pallas_call | solution.py:90
  173.6 7.0 %all-to-all-done.3 = f32[8,8,4096]{2,1,0:T(8,128)S(1)} async-done(((f32[8,8,4096]{2,1,0:T(8,128)}), f32[8,8,4096]{2,1,0:T(8,128)S(1)}, u32[]{:S(2)}, u32[]{:S(2)}) %all-to-all-start.3) | async-done | bytes 1048608 | tf_op jit(solution)/shard_map/all_to_all | solution.py:151
  180.6 7.4 %all-to-all-start.8 = ((f32[32,64,128]{2,1,0:T(8,128)}), f32[32,64,128]{2,1,0:T(8,128)S(1)}, u32[]{:S(2)}, u32[]{:S(2)}) async-start(f32[32,64,128]{2,1,0:T(8,128)} %beta.3), calls=%async_computation.8 | async-start | bytes 2097152 | tf_op jit(solution)/shard_map/all_to_all | solution.py:151
  188.0 2.8 copy-done.4
  190.8 3.1 beta.2
  193.9 23.0 %all-to-all-done.8.refs_1_ = f32[32,64,128]{2,1,0:T(8,128)S(1)} async-done(((f32[32,64,128]{2,1,0:T(8,128)}), f32[32,64,128]{2,1,0:T(8,128)S(1)}, u32[]{:S(2)}, u32[]{:S(2)}) %all-to-all-start.8) | async-done | bytes 1048608 | tf_op jit(solution)/shard_map/all_to_all | solution.py:151
  216.9 33.7 %all_to_all.69.refs_0_ = f32[32,64,128]{2,1,0:T(8,128)S(1)} all-to-all(f32[32,64,128]{2,1,0:T(8,128)S(1)} %beta.2), channel_id=1, replica_groups=mesh['op'=8,'str'=32] {'str'}, dimensions={0} | all-to-all | bytes 2097152 | tf_op jit(solution)/shard_map/all_to_all | solution.py:151
  250.7 2.8 copy-done.5
  253.4 6.5 %alpha_turned.1 = f32[128,4096]{1,0:T(8,128)} custom-call(s32[192]{0:T(256)S(1)} %reshape_squeeze.3.cols, f32[32,64,128]{2,1,0:T(8,128)S(1)} %all_to_all.69.refs_0_, f32[32,64,128]{2,1,0:T(8,128)S(1)} %all-to-all-done.8.refs_1_, bf16[32,6,128,128]{3,2,1,0:T(8,128)(2,1)S(1)} %bitcast.29), custom_call_target="tpu_custom_call" | custom-call | flops 1610612736 | bytes 10485760 | tf_op jit(solution)/shard_map/alpha_turned/pallas_call | solution.py:90
  259.9 3.6 %all-to-all-start.9 = ((f32[8,16,4096]{2,1,0:T(8,128)}), f32[8,16,4096]{2,1,0:T(8,128)S(1)}, u32[]{:S(2)}, u32[]{:S(2)}) async-start(f32[8,16,4096]{2,1,0:T(8,128)} %bitcast.12), calls=%async_computation.9 | async-start | bytes 4194304 | tf_op jit(solution)/shard_map/all_to_all | solution.py:151
  263.5 30.9 %all-to-all-done.9 = f32[8,16,4096]{2,1,0:T(8,128)S(1)} async-done(((f32[8,16,4096]{2,1,0:T(8,128)}), f32[8,16,4096]{2,1,0:T(8,128)S(1)}, u32[]{:S(2)}, u32[]{:S(2)}) %all-to-all-start.9) | async-done | bytes 2097184 | tf_op jit(solution)/shard_map/all_to_all | solution.py:151
  295.8 28.3 %all_to_all.70 = f32[8,16,4096]{2,1,0:T(8,128)S(1)} all-to-all(f32[8,16,4096]{2,1,0:T(8,128)S(1)} %broadcast_in_dim.8), channel_id=1, replica_groups=mesh['op'=8,'str'=32] {'op'}, dimensions={0} | all-to-all | bytes 4194304 | tf_op jit(solution)/shard_map/all_to_all | solution.py:151
  (20 shorter events, 6.0 us)
Async XLA Ops:
  0.9 2.8 copy-start
  3.7 1.6 copy-start.6
  51.8 33.9 %all-to-all-start.5 = ((f32[32,64,128]{2,1,0:T(8,128)}), f32[32,64,128]{2,1,0:T(8,128)S(1)}, u32[]{:S(2)}, u32[]{:S(2)}) async-start(f32[32,64,128]{2,1,0:T(8,128)} %get-tuple-element.8), calls=%async_computation.5 | async-start | bytes 2097152 | tf_op jit(solution)/shard_map/all_to_all | solution.py:151
  56.8 2.8 copy-start.1
  85.8 20.2 %all-to-all-start.1 = ((f32[8,8,4096]{2,1,0:T(8,128)}), f32[8,8,4096]{2,1,0:T(8,128)S(1)}, u32[]{:S(2)}, u32[]{:S(2)}) async-start(f32[8,8,4096]{2,1,0:T(8,128)} %bitcast.1), calls=%async_computation.1 | async-start | bytes 2097152 | tf_op jit(solution)/shard_map/all_to_all | solution.py:151
  90.8 2.8 copy-start.2
  97.5 12.8 %copy-start.7 = (f32[128,4096]{1,0:T(8,128)S(1)}, f32[128,4096]{1,0:T(8,128)}, u32[]{:S(2)}) copy-start(f32[128,4096]{1,0:T(8,128)} %field.1) | copy-start | bytes 6291460
  106.0 19.0 %all-to-all-start.6 = ((f32[8,8,4096]{2,1,0:T(8,128)}), f32[8,8,4096]{2,1,0:T(8,128)}, u32[]{:S(2)}, u32[]{:S(2)}) async-start(f32[8,8,4096]{2,1,0:T(8,128)} %bitcast.7), calls=%async_computation.6 | async-start | bytes 2097152 | tf_op jit(solution)/shard_map/all_to_all | solution.py:151
  125.0 19.2 %all-to-all-start.2 = ((f32[32,2,8,128]{3,2,1,0:T(8,128)}), f32[32,2,8,128]{3,2,1,0:T(8,128)S(1)}, u32[]{:S(2)}, u32[]{:S(2)}) async-start(f32[32,2,8,128]{3,2,1,0:T(8,128)} %turn.1), calls=%async_computation.2 | async-start | bytes 524288 | tf_op jit(solution)/shard_map/all_to_all | solution.py:151
  163.2 17.4 %all-to-all-start.3 = ((f32[8,8,4096]{2,1,0:T(8,128)}), f32[8,8,4096]{2,1,0:T(8,128)S(1)}, u32[]{:S(2)}, u32[]{:S(2)}) async-start(f32[8,8,4096]{2,1,0:T(8,128)} %broadcast_in_dim.6), calls=%async_computation.3 | async-start | bytes 2097152 | tf_op jit(solution)/shard_map/all_to_all | solution.py:151
  166.8 2.8 copy-start.3
  180.6 36.3 %all-to-all-start.8 = ((f32[32,64,128]{2,1,0:T(8,128)}), f32[32,64,128]{2,1,0:T(8,128)S(1)}, u32[]{:S(2)}, u32[]{:S(2)}) async-start(f32[32,64,128]{2,1,0:T(8,128)} %beta.3), calls=%async_computation.8 | async-start | bytes 2097152 | tf_op jit(solution)/shard_map/all_to_all | solution.py:151
  188.0 2.8 copy-start.4
  250.7 2.8 copy-start.5
  259.9 34.5 %all-to-all-start.9 = ((f32[8,16,4096]{2,1,0:T(8,128)}), f32[8,16,4096]{2,1,0:T(8,128)S(1)}, u32[]{:S(2)}, u32[]{:S(2)}) async-start(f32[8,16,4096]{2,1,0:T(8,128)} %bitcast.12), calls=%async_computation.9 | async-start | bytes 4194304 | tf_op jit(solution)/shard_map/all_to_all | solution.py:151

commit v2 on v0

v2 whole, which is shorter than its diff:
```python
import functools
import math

import jax
import jax.numpy as jnp
from jax import lax
from jax.experimental import pallas as pl
from jax.experimental.pallas import tpu as pltpu
from jax.sharding import PartitionSpec as P

BLOCK = 128
GROUP = 8
VMEM_LIMIT = 56 << 20
ROWS_BY_ROWS = (((1,), (1,)), ((), ()))
ROWS_BY_COLUMNS = (((1,), (0,)), ((), ()))


def halves_of(values):
    high = values.astype(jnp.bfloat16)
    return high, (values - high.astype(jnp.float32)).astype(jnp.bfloat16)


def block_of(c):
    return pl.ds(pl.multiple_of(c * BLOCK, BLOCK), BLOCK)


def prepare(held, axis, fetch):
    def one(c, carry):
        held[c] = jnp.concatenate(halves_of(fetch(c)), axis=axis)
        return carry

    lax.fori_loop(0, held.shape[0], one, 0, unroll=4)


def picked(cols, held, r, axis):
    return jnp.concatenate([held[cols[0, r, j]] for j in range(cols.shape[2])], axis=axis)


def product(left, right, dims):
    return lax.dot_general(left, right, dims, preferred_element_type=jnp.float32)


def first_beta(cols, field, before, out, held):
    prepare(held, 0, lambda c: field[:, block_of(c)])

    def multiply(r, factor):
        both = product(factor, picked(cols, held, r, 1), ROWS_BY_ROWS)
        out[r, :BLOCK] = both[:, :BLOCK] + both[:, BLOCK:]
        out[r, BLOCK:] = before[:, block_of(r)]

    return multiply


def first_alpha(cols, field, out, held):
    prepare(held, 0, lambda c: field[c, :BLOCK])

    def multiply(r, factor):
        both = product(factor, picked(cols, held, r, 1), ROWS_BY_ROWS)
        total = both[:, :BLOCK] + both[:, BLOCK:]
        share = out.shape[2]
        for w in range(out.shape[0]):
            out[w, r] = total[w * share : (w + 1) * share]

    return multiply


def second_alpha(cols, field, out, held):
    prepare(held, 1, lambda c: jnp.concatenate([field[w, c] for w in range(field.shape[0])], axis=0))

    def multiply(r, factor):
        both = product(factor, picked(cols, held, r, 0), ROWS_BY_COLUMNS)
        out[r] = both[:, :BLOCK] + both[:, BLOCK:]

    return multiply


def second_beta(cols, field, out, held):
    prepare(held, 0, lambda c: field[c])

    def multiply(r, factor):
        both = product(picked(cols, held, r, 1), factor, ROWS_BY_ROWS)
        out[:, block_of(r)] = both[:BLOCK] + both[BLOCK:]

    return multiply


def with_factors(body, cols, factors, *refs):
    rest, local, landed = refs[:-2], refs[-2], refs[-1]
    groups, per_group, slots = local.shape[:3]

    def copy(g):
        return pltpu.make_async_copy(factors.at[0, pl.ds(g * per_group, per_group)], local.at[g], landed.at[g])

    for g in range(groups):
        copy(g).start()
    multiply = body(cols, *rest)

    def one(g, carry):
        copy(g).wait()
        for i in range(per_group):
            multiply(g * per_group + i, jnp.concatenate([local[g, i, j] for j in range(slots)], axis=1))
        return carry

    lax.fori_loop(0, groups, one, 0)


def side(body, cols, factors, fields, out, columns=False):
    blocks, slots = factors.shape[1:3]
    groups = blocks // GROUP
    in_vmem = pl.BlockSpec(memory_space=pltpu.VMEM)
    held = (blocks, BLOCK, 2 * BLOCK) if columns else (blocks, 2 * BLOCK, BLOCK)
    return pl.pallas_call(
        functools.partial(with_factors, body),
        out_shape=jax.ShapeDtypeStruct(out, jnp.float32),
        in_specs=[pl.BlockSpec(memory_space=pltpu.SMEM), pl.BlockSpec(memory_space=pl.ANY)]
        + [in_vmem] * len(fields),
        out_specs=in_vmem,
        scratch_shapes=[
            pltpu.VMEM(held, jnp.bfloat16),
            pltpu.VMEM((groups, GROUP, slots, BLOCK, BLOCK), jnp.bfloat16),
            pltpu.SemaphoreType.DMA((groups,)),
        ],
        compiler_params=pltpu.CompilerParams(vmem_limit_bytes=VMEM_LIMIT),
        cost_estimate=pl.CostEstimate(
            flops=4 * BLOCK * blocks * slots * BLOCK * BLOCK,
            bytes_accessed=factors.size * 2 + 8 * BLOCK * blocks * BLOCK,
            transcendentals=0,
        ),
        name=body.__name__,
    )(cols, factors, *fields)


def exchange(blocks, axis):
    return lax.all_to_all(blocks, axis, 0, 0, tiled=True)


def spread(piece, shares):
    return exchange(jnp.broadcast_to(piece[None], (shares, *piece.shape)), "op")


def per_device(coeffs, previous, block_values, block_cols):
    shares = lax.axis_size("op")
    step_scale = 2.0 / math.sqrt(block_values.shape[0] * shares)
    rows, width = coeffs.shape
    blocks = block_values.shape[1]
    share = rows // shares
    start = lax.axis_index("op") * share

    def own_rows(field):
        return lax.dynamic_slice_in_dim(field, start, share, 0)

    beta = side(
        first_beta, block_cols, block_values, [coeffs, own_rows(previous)], (blocks, rows + share, BLOCK)
    )
    received = exchange(beta, "str")
    part = side(first_alpha, block_cols, block_values, [received], (shares, blocks, share, BLOCK))
    total = jnp.sum(exchange(part, "op"), axis=0)
    current = spread(step_scale * total - received[:, rows:], shares)
    alpha = side(second_alpha, block_cols, block_values, [current], (blocks, rows, BLOCK), True)
    received = exchange(alpha, "str")
    part = side(second_beta, block_cols, block_values, [received], (rows, width))
    total = jnp.sum(exchange(part.reshape(shares, share, width), "op"), axis=0)
    return spread(step_scale * total - own_rows(coeffs), shares).reshape(rows, width)


def solution(mesh):
    placed = (P("str", None), P("str", None), P("op", None, None, None, None), P("op", None, None))
    return jax.shard_map(
        per_device, mesh=mesh, in_specs=placed, out_specs=P("str", None), check_vma=False
    )
```

time: 513 us -> 289 us (0.56); the launches traced: 505 us -> 288 us
  waiting for transfers between devices: 263 us -> 0 us
  blocking collectives: 61.8 us -> 245 us
  matrix products: 56 us -> 0 us
  other arithmetic: 47 us -> 5.46 us
  local copies, waits for them, and re-layouts: 40.2 us -> 4.01 us
  Pallas kernels: 0 us -> 33.1 us
  starting transfers between devices: 23.3 us -> 0 us
  between operations: 13.7 us -> 0.07 us
    psum x2 -> x0, waiting for transfers between devices: 196 us -> none  [per_device(): updated = step_scale * lax.psum(summed, 'op') - earlier]
    all_to_all x1 -> x6, blocking collectives: 61.8 us -> 245 us  [exchange(): return lax.all_to_all(blocks, axis, 0, 0, tiled=True)]
    all_to_all x3 -> x0, waiting for transfers between devices: 66.8 us -> none  [the longest x1 47.1 us: per_device(): lax.all_to_all(beta_side, STR, split_axis=1, concat_axis=0, tiled=True)]
    dot_general x4 -> x0, matrix products: 56 us -> none  [the longest x2 29.4 us: per_device(): jnp.einsum('rjoc,rjcnm->nmro', term_factors, grouped, precision=lax.Preci...]
    select_n x5 -> x0, other arithmetic: 40.1 us -> none  [the longest x3 20 us: per_device(): jnp.take(received.reshape(block_count, block_size, group_count, item_coun...]
    pallas_call x0 -> x4, Pallas kernels: none -> 33.1 us  [side(): pl.pallas_call(functools.partial(with_factors, body), out_shape=jax.Shape...]
    gather x4 -> x0, local copies, waits for them, and re-layouts: 23.6 us -> none  [the longest x2 11.8 us: per_device(): jnp.take(current.reshape(row_count, block_count, block_size), column_list...]
    all_to_all x3 -> x0, starting transfers between devices: 22.6 us -> none  [the longest x1 11.7 us: per_device(): lax.all_to_all(beta_side, STR, split_axis=1, concat_axis=0, tiled=True)]
  transfers between devices with their start and end apart: 5 -> 0, of which waited for: 4 -> 0; matrix products, arithmetic and copies ran while one was open for 13% -> 0% of each run, Pallas kernels for 0% -> 0%
where the time goes in v2:
time: 289 us; the launch traced here: 288 us
  blocking collectives  245 us (85%)
  Pallas kernels  33.1 us (11%)
  other arithmetic  5.46 us (2%)
  local copies, waits for them, and re-layouts  4.01 us (1%)
    all_to_all x6, blocking collectives, exchange(): return lax.all_to_all(blocks, axis, 0, 0, tiled=True)  245 us
    pallas_call x4, Pallas kernels, side(): pl.pallas_call(functools.partial(with_factors, body), out_shape=jax.Shape...  33.1 us

profile of v2, /device:TPU:16, one launch (start us, length us, event | category | flops | bytes accessed | tf_op | source)
XLA Modules:
  0.0 288.0 jit_solution(3138308211866186121)
XLA Ops:
  0.0 0.0 copy-start
  0.0 1.5 copy.8.cols
  1.5 0.1 copy-done
  1.6 0.7 constant_dynamic-slice_fusion.refs_1_
  2.3 9.0 %first_beta.1 = f32[32,144,128]{2,1,0:T(8,128)} custom-call(s32[1,32,6]{2,1,0:T(8,128)} %copy.8.cols, bf16[1,32,6,128,128]{4,3,2,1,0:T(8,128)(2,1)} %factors.7, f32[128,4096]{1,0:T(8,128)} %refs_0_.1, f32[16,4096]{1,0:T(8,128)} %constant_dynamic-slice_fusion.refs_1_), custom_call_target="tpu_custom_call" | custom-call | flops 1610612736 | bytes 10485760 | tf_op jit(solution)/shard_map/first_beta/pallas_call | solution.py:112
  11.3 68.7 %all_to_all.30.refs_0_ = f32[32,144,128]{2,1,0:T(8,128)} all-to-all(f32[32,144,128]{2,1,0:T(8,128)} %first_beta.1), channel_id=1, replica_groups=mesh['op'=8,'str'=32] {'str'}, dimensions={0} | all-to-all | bytes 4718592 | tf_op jit(solution)/shard_map/all_to_all | solution.py:134
  80.1 9.0 %first_alpha.1 = f32[8,32,16,128]{3,2,1,0:T(8,128)} custom-call(s32[1,32,6]{2,1,0:T(8,128)} %copy.8.cols, bf16[1,32,6,128,128]{4,3,2,1,0:T(8,128)(2,1)} %factors.7, f32[32,144,128]{2,1,0:T(8,128)} %all_to_all.30.refs_0_), custom_call_target="tpu_custom_call" | custom-call | flops 1610612736 | bytes 10485760 | tf_op jit(solution)/shard_map/first_alpha/pallas_call | solution.py:112
  89.1 31.9 %all_to_all.31 = f32[8,32,16,128]{3,2,1,0:T(8,128)} all-to-all(f32[8,32,16,128]{3,2,1,0:T(8,128)} %first_alpha.1), channel_id=1, replica_groups=mesh['op'=8,'str'=32] {'op'}, dimensions={0} | all-to-all | bytes 4194304 | tf_op jit(solution)/shard_map/all_to_all | solution.py:134
  121.0 1.8 reduce_sum.18
  122.8 1.0 slice_subtract_fusion
  123.8 0.2 broadcast_in_dim.4
  123.9 29.0 %all_to_all.32.refs_0_ = f32[8,32,16,128]{3,2,1,0:T(8,128)} all-to-all(f32[8,32,16,128]{3,2,1,0:T(8,128)S(1)} %broadcast_in_dim.4), channel_id=1, replica_groups=mesh['op'=8,'str'=32] {'op'}, dimensions={0} | all-to-all | bytes 4194304 | tf_op jit(solution)/shard_map/all_to_all | solution.py:134
  152.9 6.7 %second_alpha.1 = f32[32,128,128]{2,1,0:T(8,128)} custom-call(s32[1,32,6]{2,1,0:T(8,128)} %copy.8.cols, bf16[1,32,6,128,128]{4,3,2,1,0:T(8,128)(2,1)} %factors.7, f32[8,32,16,128]{3,2,1,0:T(8,128)} %all_to_all.32.refs_0_), custom_call_target="tpu_custom_call" | custom-call | flops 1610612736 | bytes 10485760 | tf_op jit(solution)/shard_map/second_alpha/pallas_call | solution.py:112
  159.7 56.5 %all_to_all.33.refs_0_ = f32[32,128,128]{2,1,0:T(8,128)} all-to-all(f32[32,128,128]{2,1,0:T(8,128)} %second_alpha.1), channel_id=1, replica_groups=mesh['op'=8,'str'=32] {'str'}, dimensions={0} | all-to-all | bytes 4194304 | tf_op jit(solution)/shard_map/all_to_all | solution.py:134
  216.2 8.3 %second_beta.1 = f32[128,4096]{1,0:T(8,128)} custom-call(s32[1,32,6]{2,1,0:T(8,128)} %copy.8.cols, bf16[1,32,6,128,128]{4,3,2,1,0:T(8,128)(2,1)} %factors.7, f32[32,128,128]{2,1,0:T(8,128)} %all_to_all.33.refs_0_), custom_call_target="tpu_custom_call" | custom-call | flops 1610612736 | bytes 10485760 | tf_op jit(solution)/shard_map/second_beta/pallas_call | solution.py:112
  224.5 30.9 %all_to_all.34 = f32[8,16,4096]{2,1,0:T(8,128)} all-to-all(f32[8,16,4096]{2,1,0:T(8,128)} %bitcast.2), channel_id=1, replica_groups=mesh['op'=8,'str'=32] {'op'}, dimensions={0} | all-to-all | bytes 4194304 | tf_op jit(solution)/shard_map/all_to_all | solution.py:134
  255.4 1.7 reduce_sum.19
  257.1 1.0 dynamic-slice_subtract_fusion
  258.1 0.2 broadcast_in_dim.5
  258.3 28.4 %all_to_all.35 = f32[8,16,4096]{2,1,0:T(8,128)S(1)} all-to-all(f32[8,16,4096]{2,1,0:T(8,128)S(1)} %broadcast_in_dim.5), channel_id=1, replica_groups=mesh['op'=8,'str'=32] {'op'}, dimensions={0} | all-to-all | bytes 4194304 | tf_op jit(solution)/shard_map/all_to_all | solution.py:134
  286.7 1.3 copy.10
Async XLA Ops:
  0.0 1.6 copy-start

commit v3 on v2

v3 whole, which is shorter than its diff:
```python
import functools
import math

import jax
import jax.numpy as jnp
from jax import lax
from jax.experimental import pallas as pl
from jax.experimental.pallas import tpu as pltpu
from jax.sharding import PartitionSpec as P

BLOCK = 128
GROUP = 8
VMEM_LIMIT = 56 << 20


def halves_of(values):
    high = values.astype(jnp.bfloat16)
    return high, (values - high.astype(jnp.float32)).astype(jnp.bfloat16)


def side_kernel(turn, write, cols, factors, field, *refs):
    extra, (out, held, blocks, fields, results, semaphores) = refs[:-6], refs[-6:]
    groups, per_group, slots = blocks.shape[:3]

    def read_field(g):
        if len(field.shape) == 2:
            part = field.at[:, pl.ds(g * per_group * BLOCK, per_group * BLOCK)]
        elif len(field.shape) == 3:
            part = field.at[pl.ds(g * per_group, per_group), :BLOCK]
        else:
            part = field.at[:, pl.ds(g * per_group, per_group)]
        return pltpu.make_async_copy(part, fields.at[g], semaphores.at[0, g])

    def read_factors(g):
        part = factors.at[0, pl.ds(g * per_group, per_group)]
        return pltpu.make_async_copy(part, blocks.at[g], semaphores.at[1, g])

    def write_out(g):
        if len(out.shape) == 2:
            part = out.at[:, pl.ds(pl.multiple_of(g * per_group * BLOCK, BLOCK), per_group * BLOCK)]
        elif len(out.shape) == 3:
            part = out.at[pl.ds(g * per_group, per_group)]
        else:
            part = out.at[:, pl.ds(g * per_group, per_group)]
        return pltpu.make_async_copy(results.at[g], part, semaphores.at[2, g])

    for g in range(groups):
        read_field(g).start()
    for g in range(groups):
        read_factors(g).start()
    for g in range(groups):
        read_field(g).wait()
        for i in range(per_group):
            if len(field.shape) == 2:
                block = fields[g, :, i * BLOCK : (i + 1) * BLOCK]
            elif len(field.shape) == 3:
                block = fields[g, i]
            else:
                block = jnp.concatenate([fields[g, w, i] for w in range(field.shape[0])], axis=0)
            if turn:
                block = block.T
            held[g * per_group + i] = jnp.concatenate(halves_of(block), axis=1)

    def one(g, carry):
        read_factors(g).wait()
        for i in range(per_group):
            r = g * per_group + i
            factor = jnp.concatenate([blocks[g, i, j] for j in range(slots)], axis=1)
            picked = jnp.concatenate([held[cols[j, 0, r]] for j in range(slots)], axis=0)
            both = jnp.dot(factor, picked, preferred_element_type=jnp.float32)
            write(results, g, i, r, both[:, :BLOCK] + both[:, BLOCK:], *extra)
        write_out(g).start()
        return carry

    lax.fori_loop(0, groups, one, 0)
    for g in range(groups):
        write_out(g).wait()


def write_block(results, g, i, r, total):
    results[g, i] = total


def write_with_share(results, g, i, r, total, before):
    results[g, i, :BLOCK] = total
    results[g, i, BLOCK:] = before[:, pl.ds(pl.multiple_of(r * BLOCK, BLOCK), BLOCK)]


def write_pieces(results, g, i, r, total):
    share = results.shape[3]
    for w in range(results.shape[1]):
        results[g, w, i] = total[w * share : (w + 1) * share]


def write_turned(results, g, i, r, total):
    results[g, :, i * BLOCK : (i + 1) * BLOCK] = total.T


def grouped(shape, groups):
    if len(shape) == 2:
        return (groups, shape[0], shape[1] // groups)
    if len(shape) == 3:
        return (groups, shape[0] // groups, *shape[1:])
    return (groups, shape[0], shape[1] // groups, *shape[2:])


def side(name, turn, write, cols, factors, field, out, *extra):
    blocks, slots = factors.shape[1:3]
    groups = blocks // GROUP
    anywhere = pl.BlockSpec(memory_space=pl.ANY)
    read = field.shape if len(field.shape) != 3 else (blocks, BLOCK, BLOCK)
    return pl.pallas_call(
        functools.partial(side_kernel, turn, write),
        out_shape=jax.ShapeDtypeStruct(out, jnp.float32),
        in_specs=[pl.BlockSpec(memory_space=pltpu.SMEM), anywhere, anywhere]
        + [pl.BlockSpec(memory_space=pltpu.VMEM)] * len(extra),
        out_specs=anywhere,
        scratch_shapes=[
            pltpu.VMEM((blocks, BLOCK, 2 * BLOCK), jnp.bfloat16),
            pltpu.VMEM((groups, GROUP, slots, BLOCK, BLOCK), jnp.bfloat16),
            pltpu.VMEM(grouped(read, groups), jnp.float32),
            pltpu.VMEM(grouped(out, groups), jnp.float32),
            pltpu.SemaphoreType.DMA((3, groups)),
        ],
        compiler_params=pltpu.CompilerParams(vmem_limit_bytes=VMEM_LIMIT),
        cost_estimate=pl.CostEstimate(
            flops=4 * BLOCK * blocks * slots * BLOCK * BLOCK,
            bytes_accessed=factors.size * 2 + 8 * BLOCK * blocks * BLOCK,
            transcendentals=0,
        ),
        name=name,
    )(cols, factors, field, *extra)


def exchange(blocks, axis):
    return lax.all_to_all(blocks, axis, 0, 0, tiled=True)


def spread(piece, shares):
    return exchange(jnp.broadcast_to(piece[None], (shares, *piece.shape)), "op")


def per_device(coeffs, previous, block_values, block_cols):
    shares = lax.axis_size("op")
    step_scale = 2.0 / math.sqrt(block_values.shape[0] * shares)
    rows, width = coeffs.shape
    blocks = block_values.shape[1]
    share = rows // shares
    start = lax.axis_index("op") * share

    def own_rows(field):
        return lax.dynamic_slice_in_dim(field, start, share, 0)

    def combined(parts, earlier):
        received = exchange(parts, "op")
        total = received[0]
        for w in range(1, shares):
            total = total + received[w]
        return spread(step_scale * total - earlier, shares)

    operators = (block_cols.transpose(2, 0, 1), block_values)
    sent = side(
        "first_right", True, write_with_share, *operators, coeffs, (blocks, rows + share, BLOCK), own_rows(previous)
    )
    received = exchange(sent, "str")
    parts = side("first_left", True, write_pieces, *operators, received, (shares, blocks, share, BLOCK))
    current = combined(parts, received[:, rows:])
    sent = side("second_left", False, write_block, *operators, current, (blocks, rows, BLOCK))
    received = exchange(sent, "str")
    parts = side("second_right", True, write_turned, *operators, received, (rows, width))
    return combined(parts.reshape(shares, share, width), own_rows(coeffs)).reshape(rows, width)


def solution(mesh):
    placed = (P("str", None), P("str", None), P("op", None, None, None, None), P("op", None, None))
    return jax.shard_map(
        per_device, mesh=mesh, in_specs=placed, out_specs=P("str", None), check_vma=False
    )
```

time: 289 us -> 276 us (0.955)
  Pallas kernels: 33.1 us -> 24.8 us
  other arithmetic: 5.46 us -> 2.16 us
    pallas_call x4, Pallas kernels: 33.1 us -> 24.8 us  [side(): pl.pallas_call(functools.partial(side_kernel, turn, write), out_shape=jax...]
    reduce_sum x2 -> x0, other arithmetic: 3.47 us -> none  [the longest x1 1.75 us: per_device(): total = jnp.sum(exchange(part, 'op'), axis=0)]
where the time goes in v3:
time: 276 us; the launch traced here: 275 us
  blocking collectives  244 us (88%)
  Pallas kernels  24.8 us (9%)
  local copies, waits for them, and re-layouts  4 us (1%)
    all_to_all x6, blocking collectives, exchange(): return lax.all_to_all(blocks, axis, 0, 0, tiled=True)  244 us
    pallas_call x4, Pallas kernels, side(): pl.pallas_call(functools.partial(side_kernel, turn, write), out_shape=jax...  24.8 us

profile of v3, /device:TPU:16, one launch (start us, length us, event | category | flops | bytes accessed | tf_op | source)
XLA Modules:
  0.0 275.5 jit_solution(17045678777518544109)
XLA Ops:
  0.0 0.0 copy-start
  0.0 1.6 copy-done
  1.6 0.7 constant_dynamic-slice_fusion.refs_0_
  2.3 6.4 %first_right.1 = f32[32,144,128]{2,1,0:T(8,128)} custom-call(s32[6,1,32]{2,1,0:T(1,128)} %bitcast.13, bf16[1,32,6,128,128]{4,3,2,1,0:T(8,128)(2,1)} %factors.7, f32[128,4096]{1,0:T(8,128)} %field.1, f32[16,4096]{1,0:T(8,128)} %constant_dynamic-slice_fusion.refs_0_), custom_call_target="tpu_custom_call" | custom-call | flops 1610612736 | bytes 10485760 | tf_op jit(solution)/shard_map/first_right/pallas_call | solution.py:112
  8.7 68.7 %all_to_all.30.field = f32[32,144,128]{2,1,0:T(8,128)} all-to-all(f32[32,144,128]{2,1,0:T(8,128)} %first_right.1), channel_id=1, replica_groups=mesh['op'=8,'str'=32] {'str'}, dimensions={0} | all-to-all | bytes 4718592 | tf_op jit(solution)/shard_map/all_to_all | solution.py:136
  77.4 6.0 %first_left.1 = f32[8,32,16,128]{3,2,1,0:T(8,128)} custom-call(s32[6,1,32]{2,1,0:T(1,128)} %bitcast.14, bf16[1,32,6,128,128]{4,3,2,1,0:T(8,128)(2,1)} %factors.7, f32[32,144,128]{2,1,0:T(8,128)} %all_to_all.30.field), custom_call_target="tpu_custom_call" | custom-call | flops 1610612736 | bytes 10485760 | tf_op jit(solution)/shard_map/first_left/pallas_call | solution.py:112
  83.5 31.8 %all_to_all.31 = f32[8,32,16,128]{3,2,1,0:T(8,128)S(1)} all-to-all(f32[8,32,16,128]{3,2,1,0:T(8,128)} %first_left.1), channel_id=1, replica_groups=mesh['op'=8,'str'=32] {'op'}, dimensions={0} | all-to-all | bytes 4194304 | tf_op jit(solution)/shard_map/all_to_all | solution.py:136
  115.3 1.1 slice_subtract_fusion
  116.4 0.2 broadcast_in_dim.4
  116.6 29.0 %all_to_all.32.field = f32[8,32,16,128]{3,2,1,0:T(8,128)} all-to-all(f32[8,32,16,128]{3,2,1,0:T(8,128)S(1)} %broadcast_in_dim.4), channel_id=1, replica_groups=mesh['op'=8,'str'=32] {'op'}, dimensions={0} | all-to-all | bytes 4194304 | tf_op jit(solution)/shard_map/all_to_all | solution.py:136
  145.6 6.0 %second_left.1 = f32[32,128,128]{2,1,0:T(8,128)} custom-call(s32[6,1,32]{2,1,0:T(1,128)} %bitcast.15, bf16[1,32,6,128,128]{4,3,2,1,0:T(8,128)(2,1)} %factors.7, f32[8,32,16,128]{3,2,1,0:T(8,128)} %all_to_all.32.field), custom_call_target="tpu_custom_call" | custom-call | flops 1610612736 | bytes 10485760 | tf_op jit(solution)/shard_map/second_left/pallas_call | solution.py:112
  151.6 56.5 %all_to_all.33.field = f32[32,128,128]{2,1,0:T(8,128)} all-to-all(f32[32,128,128]{2,1,0:T(8,128)} %second_left.1), channel_id=1, replica_groups=mesh['op'=8,'str'=32] {'str'}, dimensions={0} | all-to-all | bytes 4194304 | tf_op jit(solution)/shard_map/all_to_all | solution.py:136
  208.1 6.3 %second_right.1 = f32[128,4096]{1,0:T(8,128)} custom-call(s32[6,1,32]{2,1,0:T(1,128)} %bitcast.16, bf16[1,32,6,128,128]{4,3,2,1,0:T(8,128)(2,1)} %factors.7, f32[32,128,128]{2,1,0:T(8,128)} %all_to_all.33.field), custom_call_target="tpu_custom_call" | custom-call | flops 1610612736 | bytes 10485760 | tf_op jit(solution)/shard_map/second_right/pallas_call | solution.py:112
  214.4 30.1 %all_to_all.34 = f32[8,16,4096]{2,1,0:T(8,128)S(1)} all-to-all(f32[8,16,4096]{2,1,0:T(8,128)} %bitcast.12), channel_id=1, replica_groups=mesh['op'=8,'str'=32] {'op'}, dimensions={0} | all-to-all | bytes 4194304 | tf_op jit(solution)/shard_map/all_to_all | solution.py:136
  244.5 1.1 fusion.2
  245.6 0.2 broadcast_in_dim.5
  245.8 28.4 %all_to_all.35 = f32[8,16,4096]{2,1,0:T(8,128)S(1)} all-to-all(f32[8,16,4096]{2,1,0:T(8,128)S(1)} %broadcast_in_dim.5), channel_id=1, replica_groups=mesh['op'=8,'str'=32] {'op'}, dimensions={0} | all-to-all | bytes 4194304 | tf_op jit(solution)/shard_map/all_to_all | solution.py:136
  274.2 1.3 copy.6
Async XLA Ops:
  0.0 1.6 copy-start

commit v4 on v3

--- a/solution.py
+++ b/solution.py
@@ -10,7 +10,7 @@
 
 BLOCK = 128
 GROUP = 8
-VMEM_LIMIT = 56 << 20
+VMEM_LIMIT = 24 << 20
 
 
 def halves_of(values):
@@ -18,9 +18,16 @@
     return high, (values - high.astype(jnp.float32)).astype(jnp.bfloat16)
 
 
-def side_kernel(turn, write, cols, factors, field, *refs):
-    extra, (out, held, blocks, fields, results, semaphores) = refs[:-6], refs[-6:]
-    groups, per_group, slots = blocks.shape[:3]
+def side_kernel(turn, write, fill, cols, factors, field, *refs):
+    extra, refs = refs[: len(refs) - (6 if fill else 5)], refs[len(refs) - (6 if fill else 5) :]
+    if fill:
+        out, table, held, fields, results, semaphores = refs
+    else:
+        table = factors
+        out, held, fields, results, semaphores = refs
+    groups = results.shape[0]
+    blocks, slots = table.shape[:2]
+    per_group = blocks // groups
 
     def read_field(g):
         if len(field.shape) == 2:
@@ -32,8 +39,8 @@
         return pltpu.make_async_copy(part, fields.at[g], semaphores.at[0, g])
 
     def read_factors(g):
-        part = factors.at[0, pl.ds(g * per_group, per_group)]
-        return pltpu.make_async_copy(part, blocks.at[g], semaphores.at[1, g])
+        part = pl.ds(g * per_group, per_group)
+        return pltpu.make_async_copy(factors.at[0, part], table.at[part], semaphores.at[1, g])
 
     def write_out(g):
         if len(out.shape) == 2:
@@ -46,8 +53,9 @@
 
     for g in range(groups):
         read_field(g).start()
-    for g in range(groups):
-        read_factors(g).start()
+    if fill:
+        for g in range(groups):
+            read_factors(g).start()
     for g in range(groups):
         read_field(g).wait()
         for i in range(per_group):
@@ -62,10 +70,11 @@
             held[g * per_group + i] = jnp.concatenate(halves_of(block), axis=1)
 
     def one(g, carry):
-        read_factors(g).wait()
+        if fill:
+            read_factors(g).wait()
         for i in range(per_group):
             r = g * per_group + i
-            factor = jnp.concatenate([blocks[g, i, j] for j in range(slots)], axis=1)
+            factor = jnp.concatenate([table[r, j] for j in range(slots)], axis=1)
             picked = jnp.concatenate([held[cols[j, 0, r]] for j in range(slots)], axis=0)
             both = jnp.dot(factor, picked, preferred_element_type=jnp.float32)
             write(results, g, i, r, both[:, :BLOCK] + both[:, BLOCK:], *extra)
@@ -105,19 +114,23 @@
 
 
 def side(name, turn, write, cols, factors, field, out, *extra):
-    blocks, slots = factors.shape[1:3]
+    fill = len(factors.shape) == 5
+    blocks, slots = factors.shape[-4:-2]
     groups = blocks // GROUP
     anywhere = pl.BlockSpec(memory_space=pl.ANY)
+    in_vmem = pl.BlockSpec(memory_space=pltpu.VMEM)
     read = field.shape if len(field.shape) != 3 else (blocks, BLOCK, BLOCK)
+    outs = [jax.ShapeDtypeStruct(out, jnp.float32)]
+    if fill:
+        outs.append(pltpu.VMEM((blocks, slots, BLOCK, BLOCK), jnp.bfloat16))
     return pl.pallas_call(
-        functools.partial(side_kernel, turn, write),
-        out_shape=jax.ShapeDtypeStruct(out, jnp.float32),
-        in_specs=[pl.BlockSpec(memory_space=pltpu.SMEM), anywhere, anywhere]
-        + [pl.BlockSpec(memory_space=pltpu.VMEM)] * len(extra),
-        out_specs=anywhere,
+        functools.partial(side_kernel, turn, write, fill),
+        out_shape=outs,
+        in_specs=[pl.BlockSpec(memory_space=pltpu.SMEM), anywhere if fill else in_vmem, anywhere]
+        + [in_vmem] * len(extra),
+        out_specs=[anywhere, in_vmem][: len(outs)],
         scratch_shapes=[
             pltpu.VMEM((blocks, BLOCK, 2 * BLOCK), jnp.bfloat16),
-            pltpu.VMEM((groups, GROUP, slots, BLOCK, BLOCK), jnp.bfloat16),
             pltpu.VMEM(grouped(read, groups), jnp.float32),
             pltpu.VMEM(grouped(out, groups), jnp.float32),
             pltpu.SemaphoreType.DMA((3, groups)),
@@ -158,16 +171,16 @@
             total = total + received[w]
         return spread(step_scale * total - earlier, shares)
 
-    operators = (block_cols.transpose(2, 0, 1), block_values)
-    sent = side(
-        "first_right", True, write_with_share, *operators, coeffs, (blocks, rows + share, BLOCK), own_rows(previous)
+    cols = block_cols.transpose(2, 0, 1)
+    sent, table = side(
+        "first_right", True, write_with_share, cols, block_values, coeffs, (blocks, rows + share, BLOCK), own_rows(previous)
     )
     received = exchange(sent, "str")
-    parts = side("first_left", True, write_pieces, *operators, received, (shares, blocks, share, BLOCK))
+    (parts,) = side("first_left", True, write_pieces, cols, table, received, (shares, blocks, share, BLOCK))
     current = combined(parts, received[:, rows:])
-    sent = side("second_left", False, write_block, *operators, current, (blocks, rows, BLOCK))
+    (sent,) = side("second_left", False, write_block, cols, table, current, (blocks, rows, BLOCK))
     received = exchange(sent, "str")
-    parts = side("second_right", True, write_turned, *operators, received, (rows, width))
+    (parts,) = side("second_right", True, write_turned, cols, table, received, (rows, width))
     return combined(parts.reshape(shares, share, width), own_rows(coeffs)).reshape(rows, width)
 
 

time: 276 us -> 269 us (0.975)
  Pallas kernels: 24.8 us -> 18 us
  local copies, waits for them, and re-layouts: 4 us -> 8.35 us
    pallas_call x4, Pallas kernels: 24.8 us -> 18 us  [side(): pl.pallas_call(functools.partial(side_kernel, turn, write, fill), out_sha...]
    unnamed x3 -> x9, local copies, waits for them, and re-layouts: 2.91 us -> 7.96 us
where the time goes in v4:
time: 269 us
  blocking collectives  242 us (90%)
  Pallas kernels  18 us (7%)
  local copies, waits for them, and re-layouts  8.35 us (3%)
    all_to_all x6, blocking collectives, exchange(): return lax.all_to_all(blocks, axis, 0, 0, tiled=True)  242 us
    pallas_call x4, Pallas kernels, side(): pl.pallas_call(functools.partial(side_kernel, turn, write, fill), out_sha...  18 us
    unnamed x9, local copies, waits for them, and re-layouts  7.96 us

profile of v4, /device:TPU:16, one launch (start us, length us, event | category | flops | bytes accessed | tf_op | source)
XLA Modules:
  0.0 268.7 jit_solution(473596775644202589)
XLA Ops:
  0.0 0.0 copy-start
  0.0 1.6 copy-done
  1.6 0.0 copy-start.1
  1.6 2.8 %copy-done.1 = bf16[1,32,6,128,128]{4,3,2,1,0:T(8,128)(2,1)S(1)} copy-done((bf16[1,32,6,128,128]{4,3,2,1,0:T(8,128)(2,1)S(1)}, bf16[1,32,6,128,128]{4,3,2,1,0:T(8,128)(2,1)}, u32[]{:S(2)}) %copy-start.1) | copy-done | bytes 6291480
  4.4 0.0 copy-start.2
  4.4 1.6 copy-done.2
  6.0 0.0 copy-start.3
  6.0 0.7 copy-done.3
  6.7 5.1 %first_right.1 = (f32[32,144,128]{2,1,0:T(8,128)S(1)}, bf16[32,6,128,128]{3,2,1,0:T(8,128)(2,1)S(1)}) custom-call(s32[6,1,32]{2,1,0:T(1,128)S(1)} %bitcast.12, bf16[1,32,6,128,128]{4,3,2,1,0:T(8,128)(2,1)S(1)} %copy-done.1, f32[128,4096]{1,0:T(8,128)S(1)} %copy-done.2, f32[16,4096]{1,0:T(8,128)S(1)} %constant_dynamic-slice_fusion.refs_0_), custom_call_target="tpu_custom_call" | custom-call | flops 1610612736 | bytes 10485760 | tf_op jit(solution)/shard_map/first_right/pallas_call | solution.py:126
  11.8 68.4 %all_to_all.30.field = f32[32,144,128]{2,1,0:T(8,128)S(1)} all-to-all(f32[32,144,128]{2,1,0:T(8,128)S(1)} %get-tuple-element.8), channel_id=1, replica_groups=mesh['op'=8,'str'=32] {'str'}, dimensions={0} | all-to-all | bytes 4718592 | tf_op jit(solution)/shard_map/all_to_all | solution.py:149
  80.2 4.4 %first_left.1 = f32[8,32,16,128]{3,2,1,0:T(8,128)S(1)} custom-call(s32[6,1,32]{2,1,0:T(1,128)S(1)} %bitcast.13, bf16[32,6,128,128]{3,2,1,0:T(8,128)(2,1)S(1)} %get-tuple-element.7.factors, f32[32,144,128]{2,1,0:T(8,128)S(1)} %all_to_all.30.field), custom_call_target="tpu_custom_call" | custom-call | flops 1610612736 | bytes 10485760 | tf_op jit(solution)/shard_map/first_left/pallas_call | solution.py:126
  84.6 31.6 %all_to_all.31 = f32[8,32,16,128]{3,2,1,0:T(8,128)S(1)} all-to-all(f32[8,32,16,128]{3,2,1,0:T(8,128)S(1)} %first_left.1), channel_id=1, replica_groups=mesh['op'=8,'str'=32] {'op'}, dimensions={0} | all-to-all | bytes 4194304 | tf_op jit(solution)/shard_map/all_to_all | solution.py:149
  116.2 0.2 slice_subtract_fusion
  116.4 0.2 broadcast_in_dim.4
  116.5 28.6 %all_to_all.32.field = f32[8,32,16,128]{3,2,1,0:T(8,128)S(1)} all-to-all(f32[8,32,16,128]{3,2,1,0:T(8,128)S(1)} %broadcast_in_dim.4), channel_id=1, replica_groups=mesh['op'=8,'str'=32] {'op'}, dimensions={0} | all-to-all | bytes 4194304 | tf_op jit(solution)/shard_map/all_to_all | solution.py:149
  145.1 3.8 %second_left.1 = f32[32,128,128]{2,1,0:T(8,128)S(1)} custom-call(s32[6,1,32]{2,1,0:T(1,128)S(1)} %bitcast.14, bf16[32,6,128,128]{3,2,1,0:T(8,128)(2,1)S(1)} %get-tuple-element.7.factors, f32[8,32,16,128]{3,2,1,0:T(8,128)S(1)} %all_to_all.32.field), custom_call_target="tpu_custom_call" | custom-call | flops 1610612736 | bytes 10485760 | tf_op jit(solution)/shard_map/second_left/pallas_call | solution.py:126
  148.9 56.5 %all_to_all.33.field = f32[32,128,128]{2,1,0:T(8,128)S(1)} all-to-all(f32[32,128,128]{2,1,0:T(8,128)S(1)} %second_left.1), channel_id=1, replica_groups=mesh['op'=8,'str'=32] {'str'}, dimensions={0} | all-to-all | bytes 4194304 | tf_op jit(solution)/shard_map/all_to_all | solution.py:149
  205.4 4.6 %second_right.1 = f32[128,4096]{1,0:T(8,128)S(1)} custom-call(s32[6,1,32]{2,1,0:T(1,128)S(1)} %bitcast.15, bf16[32,6,128,128]{3,2,1,0:T(8,128)(2,1)S(1)} %get-tuple-element.7.factors, f32[32,128,128]{2,1,0:T(8,128)S(1)} %all_to_all.33.field), custom_call_target="tpu_custom_call" | custom-call | flops 1610612736 | bytes 10485760 | tf_op jit(solution)/shard_map/second_right/pallas_call | solution.py:126
  210.1 29.1 %all_to_all.34 = f32[8,16,4096]{2,1,0:T(8,128)S(1)} all-to-all(f32[8,16,4096]{2,1,0:T(8,128)S(1)} %bitcast.11), channel_id=1, replica_groups=mesh['op'=8,'str'=32] {'op'}, dimensions={0} | all-to-all | bytes 4194304 | tf_op jit(solution)/shard_map/all_to_all | solution.py:149
  239.2 0.1 fusion.2
  239.3 0.2 broadcast_in_dim.5
  239.5 27.9 %all_to_all.35 = f32[8,16,4096]{2,1,0:T(8,128)S(1)} all-to-all(f32[8,16,4096]{2,1,0:T(8,128)S(1)} %broadcast_in_dim.5), channel_id=1, replica_groups=mesh['op'=8,'str'=32] {'op'}, dimensions={0} | all-to-all | bytes 4194304 | tf_op jit(solution)/shard_map/all_to_all | solution.py:149
  267.4 1.3 copy.6
  (1 shorter events, 0.0 us)
Async XLA Ops:
  0.0 1.6 copy-start
  1.6 2.8 %copy-start.1 = (bf16[1,32,6,128,128]{4,3,2,1,0:T(8,128)(2,1)S(1)}, bf16[1,32,6,128,128]{4,3,2,1,0:T(8,128)(2,1)}, u32[]{:S(2)}) copy-start(bf16[1,32,6,128,128]{4,3,2,1,0:T(8,128)(2,1)} %factors.1) | copy-start | bytes 18874372
  4.4 1.6 copy-start.2
  6.0 0.7 copy-start.3

commit v5 on v3

v5 whole, which is shorter than its diff:
```python
import functools
import math

import jax
import jax.numpy as jnp
from jax import lax
from jax.experimental import pallas as pl
from jax.experimental.pallas import tpu as pltpu
from jax.sharding import PartitionSpec as P

BLOCK = 128
GROUP = 8
VMEM_LIMIT = 24 << 20


def halves_of(values):
    high = values.astype(jnp.bfloat16)
    return high, (values - high.astype(jnp.float32)).astype(jnp.bfloat16)


def first_kernel(place, cols, factors, field, before, out, table, held, fields, share, results, landed):
    groups, per_group = results.shape[:2]
    rows = share.shape[0]

    def read_field(g):
        part = field.at[:, pl.ds(g * per_group * BLOCK, per_group * BLOCK)]
        return pltpu.make_async_copy(part, fields.at[g], landed.at[0, g])

    def read_factors(g):
        part = pl.ds(g * per_group, per_group)
        return pltpu.make_async_copy(factors.at[0, part], table.at[part], landed.at[1, g])

    def write_out(g):
        part = out.at[pl.ds(g * per_group, per_group)]
        return pltpu.make_async_copy(results.at[g], part, landed.at[2, g])

    start = pl.multiple_of(place[0] * rows, rows)
    read_before = pltpu.make_async_copy(before.at[pl.ds(start, rows)], share, landed.at[3, 0])
    for g in range(groups):
        read_field(g).start()
    read_before.start()
    for g in range(groups):
        read_factors(g).start()
    for g in range(groups):
        read_field(g).wait()
        for i in range(per_group):
            block = fields[g, :, i * BLOCK : (i + 1) * BLOCK]
            held[g * per_group + i] = jnp.concatenate(halves_of(block.T), axis=1)
    read_before.wait()

    def one(g, carry):
        read_factors(g).wait()
        for i in range(per_group):
            r = g * per_group + i
            results[g, i, :BLOCK] = product(cols, table, held, r)
            results[g, i, BLOCK:] = share[:, pl.ds(pl.multiple_of(r * BLOCK, BLOCK), BLOCK)]
        write_out(g).start()
        return carry

    lax.fori_loop(0, groups, one, 0)
    for g in range(groups):
        write_out(g).wait()


def product(cols, table, held, r):
    slots = table.shape[1]
    factor = jnp.concatenate([table[r, j] for j in range(slots)], axis=1)
    picked = jnp.concatenate([held[cols[j, 0, r]] for j in range(slots)], axis=0)
    both = jnp.dot(factor, picked, preferred_element_type=jnp.float32)
    return both[:, :BLOCK] + both[:, BLOCK:]


def later_kernel(read, write, cols, table, field, out, held):
    blocks = table.shape[0]
    for c in range(blocks):
        held[c] = jnp.concatenate(halves_of(read(field, c)), axis=1)

    def one(g, carry):
        for i in range(GROUP):
            r = g * GROUP + i
            write(out, r, product(cols, table, held, r))
        return carry

    lax.fori_loop(0, blocks // GROUP, one, 0)


def read_turned(field, c):
    return field[c, :BLOCK].T


def read_pieces(field, c):
    return jnp.concatenate([field[w, c] for w in range(field.shape[0])], axis=0)


def write_block(out, r, total):
    out[r] = total


def write_pieces(out, r, total):
    share = out.shape[2]
    for w in range(out.shape[0]):
        out[w, r] = total[w * share : (w + 1) * share]


def write_turned(out, r, total):
    out[:, pl.ds(pl.multiple_of(r * BLOCK, BLOCK), BLOCK)] = total.T


def cost(blocks, slots):
    size = blocks * BLOCK * BLOCK
    return pl.CostEstimate(flops=4 * size * slots * BLOCK, bytes_accessed=size * (2 * slots + 8), transcendentals=0)


def first_side(place, cols, factors, field, before, share):
    blocks, slots = factors.shape[1:3]
    groups = blocks // GROUP
    rows = field.shape[0]
    in_smem, in_vmem, in_hbm = (pl.BlockSpec(memory_space=m) for m in (pltpu.SMEM, pltpu.VMEM, pltpu.HBM))
    far = [pltpu.with_memory_space_constraint(x, pltpu.HBM) for x in (factors, field, before)]
    return pl.pallas_call(
        first_kernel,
        out_shape=[
            jax.ShapeDtypeStruct((blocks, rows + share, BLOCK), jnp.float32),
            pltpu.VMEM((blocks, slots, BLOCK, BLOCK), jnp.bfloat16),
        ],
        in_specs=[in_smem, in_smem, in_hbm, in_hbm, in_hbm],
        out_specs=[pl.BlockSpec(memory_space=pl.ANY), in_vmem],
        scratch_shapes=[
            pltpu.VMEM((blocks, BLOCK, 2 * BLOCK), jnp.bfloat16),
            pltpu.VMEM((groups, rows, GROUP * BLOCK), jnp.float32),
            pltpu.VMEM((share, blocks * BLOCK), jnp.float32),
            pltpu.VMEM((groups, GROUP, rows + share, BLOCK), jnp.float32),
            pltpu.SemaphoreType.DMA((4, groups)),
        ],
        compiler_params=pltpu.CompilerParams(vmem_limit_bytes=VMEM_LIMIT),
        cost_estimate=cost(blocks, slots),
        name="first_right",
    )(place, cols, *far)


def side(name, read, write, cols, table, field, out):
    blocks, slots = table.shape[:2]
    in_vmem = pl.BlockSpec(memory_space=pltpu.VMEM)
    return pl.pallas_call(
        functools.partial(later_kernel, read, write),
        out_shape=pltpu.VMEM(out, jnp.float32),
        in_specs=[pl.BlockSpec(memory_space=pltpu.SMEM), in_vmem, in_vmem],
        out_specs=in_vmem,
        scratch_shapes=[pltpu.VMEM((blocks, BLOCK, 2 * BLOCK), jnp.bfloat16)],
        compiler_params=pltpu.CompilerParams(vmem_limit_bytes=VMEM_LIMIT),
        cost_estimate=cost(blocks, slots),
        name=name,
    )(cols, table, pltpu.with_memory_space_constraint(field, pltpu.VMEM))


def exchange(blocks, axis):
    return lax.all_to_all(blocks, axis, 0, 0, tiled=True)


def spread(piece, shares):
    return exchange(jnp.broadcast_to(piece[None], (shares, *piece.shape)), "op")


def per_device(coeffs, previous, block_values, block_cols):
    shares = lax.axis_size("op")
    step_scale = 2.0 / math.sqrt(block_values.shape[0] * shares)
    rows, width = coeffs.shape
    blocks = block_values.shape[1]
    share = rows // shares
    start = lax.axis_index("op") * share

    def own_rows(field):
        return lax.dynamic_slice_in_dim(field, start, share, 0)

    def combined(parts, earlier):
        received = exchange(parts, "op")
        total = received[0]
        for w in range(1, shares):
            total = total + received[w]
        return spread(step_scale * total - earlier, shares)

    cols = block_cols.transpose(2, 0, 1)
    place = lax.axis_index("op").astype(jnp.int32).reshape(1)
    sent, table = first_side(place, cols, block_values, coeffs, previous, share)
    received = exchange(sent, "str")
    parts = side("first_left", read_turned, write_pieces, cols, table, received, (shares, blocks, share, BLOCK))
    current = combined(parts, received[:, rows:])
    sent = side("second_left", read_pieces, write_block, cols, table, current, (blocks, rows, BLOCK))
    received = exchange(sent, "str")
    parts = side("second_right", read_turned, write_turned, cols, table, received, (rows, width))
    return combined(parts.reshape(shares, share, width), own_rows(coeffs)).reshape(rows, width)


def solution(mesh):
    placed = (P("str", None), P("str", None), P("op", None, None, None, None), P("op", None, None))
    return jax.shard_map(
        per_device, mesh=mesh, in_specs=placed, out_specs=P("str", None), check_vma=False
    )
```

time: 276 us -> 270 us (0.978)
  blocking collectives: 244 us -> 213 us
  waiting for transfers between devices: 0 us -> 30.9 us
  Pallas kernels: 24.8 us -> 17.8 us
  starting transfers between devices: 0 us -> 3.6 us
    all_to_all x6 -> x5, blocking collectives: 244 us -> 213 us  [exchange(): return lax.all_to_all(blocks, axis, 0, 0, tiled=True)]
    all_to_all x0 -> x1, waiting for transfers between devices: none -> 30.9 us  [exchange(): return lax.all_to_all(blocks, axis, 0, 0, tiled=True)]
    pallas_call x4, Pallas kernels: 24.8 us -> 17.8 us  [the longest x3 12 us: side(): pl.pallas_call(functools.partial(later_kernel, read, write), out_shape=pl...]
    all_to_all x0 -> x1, starting transfers between devices: none -> 3.6 us  [exchange(): return lax.all_to_all(blocks, axis, 0, 0, tiled=True)]
  transfers between devices with their start and end apart: 0 -> 1, of which waited for: 0 -> 1; matrix products, arithmetic and copies ran while one was open for 0% -> 0% of each run, Pallas kernels for 0% -> 0%
where the time goes in v5:
time: 270 us; the launch traced here: 269 us
  blocking collectives  213 us (79%)
  waiting for transfers between devices  30.9 us (11%)
  Pallas kernels  17.8 us (7%)
  starting transfers between devices  3.6 us (1%)
    all_to_all x5, blocking collectives, exchange(): return lax.all_to_all(blocks, axis, 0, 0, tiled=True)  213 us
    all_to_all x1, waiting for transfers between devices, exchange(): return lax.all_to_all(blocks, axis, 0, 0, tiled=True)  30.9 us
    pallas_call x3, Pallas kernels, side(): pl.pallas_call(functools.partial(later_kernel, read, write), out_shape=pl...  12 us
    pallas_call x1, Pallas kernels, first_side(): pl.pallas_call(first_kernel, out_shape=[jax.ShapeDtypeStruct((blocks, row...  5.81 us
  transfers between devices with their start and end apart: 1, of which 1 were waited for; matrix products, arithmetic and copies ran while one was open for 0% of the time, Pallas kernels for 0%

profile of v5, /device:TPU:16, one launch (start us, length us, event | category | flops | bytes accessed | tf_op | source)
XLA Modules:
  0.0 269.4 jit_solution(2881452023227509232)
XLA Ops:
  0.0 0.0 copy-start
  0.0 0.7 copy-done
  0.7 5.8 %first_right.1 = (f32[32,144,128]{2,1,0:T(8,128)S(1)}, bf16[32,6,128,128]{3,2,1,0:T(8,128)(2,1)S(1)}) custom-call(s32[1]{0:T(128)} %bitcast.1.place, s32[6,1,32]{2,1,0:T(1,128)S(1)} %bitcast.12, bf16[1,32,6,128,128]{4,3,2,1,0:T(8,128)(2,1)} %factors.1, f32[128,4096]{1,0:T(8,128)} %field.1, f32[128,4096]{1,0:T(8,128)} %before.1), custom_call_target="tpu_custom_call" | custom-call | flops 1610612736 | bytes 10485760 | tf_op jit(solution)/shard_map/first_right/pallas_call | solution.py:120
  6.5 0.0 copy-start.1
  6.5 68.4 %all_to_all.30.field = f32[32,144,128]{2,1,0:T(8,128)S(1)} all-to-all(f32[32,144,128]{2,1,0:T(8,128)S(1)} %get-tuple-element.8), channel_id=1, replica_groups=mesh['op'=8,'str'=32] {'str'}, dimensions={0} | all-to-all | bytes 4718592 | tf_op jit(solution)/shard_map/all_to_all | solution.py:157
  74.9 0.0 copy-done.1
  74.9 3.6 %first_left.1 = f32[8,32,16,128]{3,2,1,0:T(8,128)S(1)} custom-call(s32[6,1,32]{2,1,0:T(1,128)S(1)} %bitcast.13, bf16[32,6,128,128]{3,2,1,0:T(8,128)(2,1)S(1)} %get-tuple-element.7.table, f32[32,144,128]{2,1,0:T(8,128)S(1)} %all_to_all.30.field), custom_call_target="tpu_custom_call" | custom-call | flops 1610612736 | bytes 10485760 | tf_op jit(solution)/shard_map/first_left/pallas_call | solution.py:144
  78.5 31.6 %all_to_all.31 = f32[8,32,16,128]{3,2,1,0:T(8,128)S(1)} all-to-all(f32[8,32,16,128]{3,2,1,0:T(8,128)S(1)} %first_left.1), channel_id=1, replica_groups=mesh['op'=8,'str'=32] {'op'}, dimensions={0} | all-to-all | bytes 4194304 | tf_op jit(solution)/shard_map/all_to_all | solution.py:157
  110.1 0.2 slice_subtract_fusion
  110.3 0.2 broadcast_in_dim.4
  110.5 28.6 %all_to_all.32.field = f32[8,32,16,128]{3,2,1,0:T(8,128)S(1)} all-to-all(f32[8,32,16,128]{3,2,1,0:T(8,128)S(1)} %broadcast_in_dim.4), channel_id=1, replica_groups=mesh['op'=8,'str'=32] {'op'}, dimensions={0} | all-to-all | bytes 4194304 | tf_op jit(solution)/shard_map/all_to_all | solution.py:157
  139.0 3.2 %second_left.1 = f32[32,128,128]{2,1,0:T(8,128)S(1)} custom-call(s32[6,1,32]{2,1,0:T(1,128)S(1)} %bitcast.14, bf16[32,6,128,128]{3,2,1,0:T(8,128)(2,1)S(1)} %get-tuple-element.7.table, f32[8,32,16,128]{3,2,1,0:T(8,128)S(1)} %all_to_all.32.field), custom_call_target="tpu_custom_call" | custom-call | flops 1610612736 | bytes 10485760 | tf_op jit(solution)/shard_map/second_left/pallas_call | solution.py:144
  142.3 56.5 %all_to_all.33.field = f32[32,128,128]{2,1,0:T(8,128)S(1)} all-to-all(f32[32,128,128]{2,1,0:T(8,128)S(1)} %second_left.1), channel_id=1, replica_groups=mesh['op'=8,'str'=32] {'str'}, dimensions={0} | all-to-all | bytes 4194304 | tf_op jit(solution)/shard_map/all_to_all | solution.py:157
  198.7 5.2 %second_right.1 = f32[128,4096]{1,0:T(8,128)} custom-call(s32[6,1,32]{2,1,0:T(1,128)S(1)} %bitcast.15, bf16[32,6,128,128]{3,2,1,0:T(8,128)(2,1)S(1)} %get-tuple-element.7.table, f32[32,128,128]{2,1,0:T(8,128)S(1)} %all_to_all.33.field), custom_call_target="tpu_custom_call" | custom-call | flops 1610612736 | bytes 10485760 | tf_op jit(solution)/shard_map/second_right/pallas_call | solution.py:144
  203.9 3.6 %all-to-all-start.4 = ((f32[8,16,4096]{2,1,0:T(8,128)}), f32[8,16,4096]{2,1,0:T(8,128)S(1)}, u32[]{:S(2)}, u32[]{:S(2)}) async-start(f32[8,16,4096]{2,1,0:T(8,128)} %bitcast.3), calls=%async_computation.4 | async-start | bytes 4194304 | tf_op jit(solution)/shard_map/all_to_all | solution.py:157
  207.6 30.9 %all-to-all-done.4 = f32[8,16,4096]{2,1,0:T(8,128)S(1)} async-done(((f32[8,16,4096]{2,1,0:T(8,128)}), f32[8,16,4096]{2,1,0:T(8,128)S(1)}, u32[]{:S(2)}, u32[]{:S(2)}) %all-to-all-start.4) | async-done | bytes 2097184 | tf_op jit(solution)/shard_map/all_to_all | solution.py:157
  238.5 1.1 fusion.2
  239.5 0.2 broadcast_in_dim.5
  239.8 28.3 %all_to_all.34 = f32[8,16,4096]{2,1,0:T(8,128)S(1)} all-to-all(f32[8,16,4096]{2,1,0:T(8,128)S(1)} %broadcast_in_dim.5), channel_id=1, replica_groups=mesh['op'=8,'str'=32] {'op'}, dimensions={0} | all-to-all | bytes 4194304 | tf_op jit(solution)/shard_map/all_to_all | solution.py:157
  268.1 1.3 copy.6
Async XLA Ops:
  0.0 0.7 copy-start
  6.5 68.4 %copy-start.1 = (s32[1,32,6]{1,0,2:T(1,128)S(1)}, s32[1,32,6]{1,0,2:T(1,128)}, u32[]{:S(2)}) copy-start(s32[1,32,6]{1,0,2:T(1,128)} %param.7) | copy-start | bytes 2308
  203.9 34.6 %all-to-all-start.4 = ((f32[8,16,4096]{2,1,0:T(8,128)}), f32[8,16,4096]{2,1,0:T(8,128)S(1)}, u32[]{:S(2)}, u32[]{:S(2)}) async-start(f32[8,16,4096]{2,1,0:T(8,128)} %bitcast.3), calls=%async_computation.4 | async-start | bytes 4194304 | tf_op jit(solution)/shard_map/all_to_all | solution.py:157

commit v6 on v5

--- a/solution.py
+++ b/solution.py
@@ -18,7 +18,7 @@
     return high, (values - high.astype(jnp.float32)).astype(jnp.bfloat16)
 
 
-def first_kernel(place, cols, factors, field, before, out, table, held, fields, share, results, landed):
+def first_kernel(place, cols, factors, field, before, out, table, kept, held, fields, share, results, landed):
     groups, per_group = results.shape[:2]
     rows = share.shape[0]
 
@@ -43,6 +43,7 @@
         read_factors(g).start()
     for g in range(groups):
         read_field(g).wait()
+        kept[:, g * per_group * BLOCK : (g + 1) * per_group * BLOCK] = fields[g, pl.ds(start, rows)]
         for i in range(per_group):
             block = fields[g, :, i * BLOCK : (i + 1) * BLOCK]
             held[g * per_group + i] = jnp.concatenate(halves_of(block.T), axis=1)
@@ -122,9 +123,10 @@
         out_shape=[
             jax.ShapeDtypeStruct((blocks, rows + share, BLOCK), jnp.float32),
             pltpu.VMEM((blocks, slots, BLOCK, BLOCK), jnp.bfloat16),
+            pltpu.VMEM((share, blocks * BLOCK), jnp.float32),
         ],
         in_specs=[in_smem, in_smem, in_hbm, in_hbm, in_hbm],
-        out_specs=[pl.BlockSpec(memory_space=pl.ANY), in_vmem],
+        out_specs=[pl.BlockSpec(memory_space=pl.ANY), in_vmem, in_vmem],
         scratch_shapes=[
             pltpu.VMEM((blocks, BLOCK, 2 * BLOCK), jnp.bfloat16),
             pltpu.VMEM((groups, rows, GROUP * BLOCK), jnp.float32),
@@ -167,10 +169,6 @@
     rows, width = coeffs.shape
     blocks = block_values.shape[1]
     share = rows // shares
-    start = lax.axis_index("op") * share
-
-    def own_rows(field):
-        return lax.dynamic_slice_in_dim(field, start, share, 0)
 
     def combined(parts, earlier):
         received = exchange(parts, "op")
@@ -181,14 +179,14 @@
 
     cols = block_cols.transpose(2, 0, 1)
     place = lax.axis_index("op").astype(jnp.int32).reshape(1)
-    sent, table = first_side(place, cols, block_values, coeffs, previous, share)
+    sent, table, kept = first_side(place, cols, block_values, coeffs, previous, share)
     received = exchange(sent, "str")
     parts = side("first_left", read_turned, write_pieces, cols, table, received, (shares, blocks, share, BLOCK))
     current = combined(parts, received[:, rows:])
     sent = side("second_left", read_pieces, write_block, cols, table, current, (blocks, rows, BLOCK))
     received = exchange(sent, "str")
     parts = side("second_right", read_turned, write_turned, cols, table, received, (rows, width))
-    return combined(parts.reshape(shares, share, width), own_rows(coeffs)).reshape(rows, width)
+    return combined(parts.reshape(shares, share, width), kept).reshape(rows, width)
 
 
 def solution(mesh):

time: 270 us -> 262 us (0.970)
  waiting for transfers between devices: 30.9 us -> 0 us
  blocking collectives: 213 us -> 242 us
  starting transfers between devices: 3.6 us -> 0 us
    all_to_all x1 -> x0, waiting for transfers between devices: 30.9 us -> none  [exchange(): return lax.all_to_all(blocks, axis, 0, 0, tiled=True)]
    all_to_all x5 -> x6, blocking collectives: 213 us -> 242 us  [exchange(): return lax.all_to_all(blocks, axis, 0, 0, tiled=True)]
    all_to_all x1 -> x0, starting transfers between devices: 3.6 us -> none  [exchange(): return lax.all_to_all(blocks, axis, 0, 0, tiled=True)]
  transfers between devices with their start and end apart: 1 -> 0, of which waited for: 1 -> 0; matrix products, arithmetic and copies ran while one was open for 0% -> 0% of each run, Pallas kernels for 0% -> 0%
where the time goes in v6:
time: 262 us
  blocking collectives  242 us (92%)
  Pallas kernels  17 us (6%)
    all_to_all x6, blocking collectives, exchange(): return lax.all_to_all(blocks, axis, 0, 0, tiled=True)  242 us
    pallas_call x3, Pallas kernels, side(): pl.pallas_call(functools.partial(later_kernel, read, write), out_shape=pl...  11.1 us
    pallas_call x1, Pallas kernels, first_side(): pl.pallas_call(first_kernel, out_shape=[jax.ShapeDtypeStruct((blocks, row...  5.92 us

profile of v6, /device:TPU:16, one launch (start us, length us, event | category | flops | bytes accessed | tf_op | source)
XLA Modules:
  0.0 261.8 jit_solution(10765256931487885637)
XLA Ops:
  0.0 0.0 copy-start
  0.0 0.7 copy-done
  0.7 5.9 %first_right.1 = (f32[32,144,128]{2,1,0:T(8,128)S(1)}, bf16[32,6,128,128]{3,2,1,0:T(8,128)(2,1)S(1)}, f32[16,4096]{1,0:T(8,128)S(1)}) custom-call(s32[1]{0:T(128)} %bitcast.1.place, s32[6,1,32]{2,1,0:T(1,128)S(1)} %bitcast.13, bf16[1,32,6,128,128]{4,3,2,1,0:T(8,128)(2,1)} %factors.1, f32[128,4096]{1,0:T(8,128)} %field.1, f32[128,4096]{1,0:T(8,128)} %before.1), custom_call_target="tpu_custom_call" | custom-call | flops 1610612736 | bytes 10485760 | tf_op jit(solution)/shard_map/first_right/pallas_call | solution.py:121
  6.6 0.0 copy-start.1
  6.6 68.4 %all_to_all.30.field = f32[32,144,128]{2,1,0:T(8,128)S(1)} all-to-all(f32[32,144,128]{2,1,0:T(8,128)S(1)} %get-tuple-element.9), channel_id=1, replica_groups=mesh['op'=8,'str'=32] {'str'}, dimensions={0} | all-to-all | bytes 4718592 | tf_op jit(solution)/shard_map/all_to_all | solution.py:159
  75.0 0.0 copy-done.1
  75.0 3.7 %first_left.1 = f32[8,32,16,128]{3,2,1,0:T(8,128)S(1)} custom-call(s32[6,1,32]{2,1,0:T(1,128)S(1)} %bitcast.14, bf16[32,6,128,128]{3,2,1,0:T(8,128)(2,1)S(1)} %get-tuple-element.8.table, f32[32,144,128]{2,1,0:T(8,128)S(1)} %all_to_all.30.field), custom_call_target="tpu_custom_call" | custom-call | flops 1610612736 | bytes 10485760 | tf_op jit(solution)/shard_map/first_left/pallas_call | solution.py:146
  78.8 31.6 %all_to_all.31 = f32[8,32,16,128]{3,2,1,0:T(8,128)S(1)} all-to-all(f32[8,32,16,128]{3,2,1,0:T(8,128)S(1)} %first_left.1), channel_id=1, replica_groups=mesh['op'=8,'str'=32] {'op'}, dimensions={0} | all-to-all | bytes 4194304 | tf_op jit(solution)/shard_map/all_to_all | solution.py:159
  110.4 0.2 slice_subtract_fusion
  110.5 0.2 broadcast_in_dim.4
  110.7 28.6 %all_to_all.32.field = f32[8,32,16,128]{3,2,1,0:T(8,128)S(1)} all-to-all(f32[8,32,16,128]{3,2,1,0:T(8,128)S(1)} %broadcast_in_dim.4), channel_id=1, replica_groups=mesh['op'=8,'str'=32] {'op'}, dimensions={0} | all-to-all | bytes 4194304 | tf_op jit(solution)/shard_map/all_to_all | solution.py:159
  139.3 3.4 %second_left.1 = f32[32,128,128]{2,1,0:T(8,128)S(1)} custom-call(s32[6,1,32]{2,1,0:T(1,128)S(1)} %bitcast.15, bf16[32,6,128,128]{3,2,1,0:T(8,128)(2,1)S(1)} %get-tuple-element.8.table, f32[8,32,16,128]{3,2,1,0:T(8,128)S(1)} %all_to_all.32.field), custom_call_target="tpu_custom_call" | custom-call | flops 1610612736 | bytes 10485760 | tf_op jit(solution)/shard_map/second_left/pallas_call | solution.py:146
  142.7 56.5 %all_to_all.33.field = f32[32,128,128]{2,1,0:T(8,128)S(1)} all-to-all(f32[32,128,128]{2,1,0:T(8,128)S(1)} %second_left.1), channel_id=1, replica_groups=mesh['op'=8,'str'=32] {'str'}, dimensions={0} | all-to-all | bytes 4194304 | tf_op jit(solution)/shard_map/all_to_all | solution.py:159
  199.1 4.0 %second_right.1 = f32[128,4096]{1,0:T(8,128)S(1)} custom-call(s32[6,1,32]{2,1,0:T(1,128)S(1)} %bitcast.16, bf16[32,6,128,128]{3,2,1,0:T(8,128)(2,1)S(1)} %get-tuple-element.8.table, f32[32,128,128]{2,1,0:T(8,128)S(1)} %all_to_all.33.field), custom_call_target="tpu_custom_call" | custom-call | flops 1610612736 | bytes 10485760 | tf_op jit(solution)/shard_map/second_right/pallas_call | solution.py:146
  203.1 29.1 %all_to_all.34 = f32[8,16,4096]{2,1,0:T(8,128)S(1)} all-to-all(f32[8,16,4096]{2,1,0:T(8,128)S(1)} %bitcast.12), channel_id=1, replica_groups=mesh['op'=8,'str'=32] {'op'}, dimensions={0} | all-to-all | bytes 4194304 | tf_op jit(solution)/shard_map/all_to_all | solution.py:159
  232.2 0.1 fusion.2
  232.4 0.2 broadcast_in_dim.5
  232.6 27.9 %all_to_all.35 = f32[8,16,4096]{2,1,0:T(8,128)S(1)} all-to-all(f32[8,16,4096]{2,1,0:T(8,128)S(1)} %broadcast_in_dim.5), channel_id=1, replica_groups=mesh['op'=8,'str'=32] {'op'}, dimensions={0} | all-to-all | bytes 4194304 | tf_op jit(solution)/shard_map/all_to_all | solution.py:159
  260.5 1.3 copy.6
Async XLA Ops:
  0.0 0.7 copy-start
  6.6 68.4 %copy-start.1 = (s32[1,32,6]{1,0,2:T(1,128)S(1)}, s32[1,32,6]{1,0,2:T(1,128)}, u32[]{:S(2)}) copy-start(s32[1,32,6]{1,0,2:T(1,128)} %param.7) | copy-start | bytes 2308

commit v7 on v6

--- a/solution.py
+++ b/solution.py
@@ -18,8 +18,9 @@
     return high, (values - high.astype(jnp.float32)).astype(jnp.bfloat16)
 
 
-def first_kernel(place, cols, factors, field, before, out, table, kept, held, fields, share, results, landed):
-    groups, per_group = results.shape[:2]
+def first_kernel(place, columns, factors, field, before, out, table, kept, cols, held, fields, share, landed):
+    groups = fields.shape[0]
+    per_group = table.shape[0] // groups
     rows = share.shape[0]
 
     def read_field(g):
@@ -30,14 +31,12 @@
         part = pl.ds(g * per_group, per_group)
         return pltpu.make_async_copy(factors.at[0, part], table.at[part], landed.at[1, g])
 
-    def write_out(g):
-        part = out.at[pl.ds(g * per_group, per_group)]
-        return pltpu.make_async_copy(results.at[g], part, landed.at[2, g])
-
     start = pl.multiple_of(place[0] * rows, rows)
-    read_before = pltpu.make_async_copy(before.at[pl.ds(start, rows)], share, landed.at[3, 0])
+    read_before = pltpu.make_async_copy(before.at[pl.ds(start, rows)], share, landed.at[2, 0])
+    read_columns = pltpu.make_async_copy(columns, cols, landed.at[2, 1])
     for g in range(groups):
         read_field(g).start()
+    read_columns.start()
     read_before.start()
     for g in range(groups):
         read_factors(g).start()
@@ -47,20 +46,18 @@
         for i in range(per_group):
             block = fields[g, :, i * BLOCK : (i + 1) * BLOCK]
             held[g * per_group + i] = jnp.concatenate(halves_of(block.T), axis=1)
+    read_columns.wait()
     read_before.wait()
 
     def one(g, carry):
         read_factors(g).wait()
         for i in range(per_group):
             r = g * per_group + i
-            results[g, i, :BLOCK] = product(cols, table, held, r)
-            results[g, i, BLOCK:] = share[:, pl.ds(pl.multiple_of(r * BLOCK, BLOCK), BLOCK)]
-        write_out(g).start()
+            out[r, :BLOCK] = product(cols, table, held, r)
+            out[r, BLOCK:] = share[:, pl.ds(pl.multiple_of(r * BLOCK, BLOCK), BLOCK)]
         return carry
 
     lax.fori_loop(0, groups, one, 0)
-    for g in range(groups):
-        write_out(g).wait()
 
 
 def product(cols, table, held, r):
@@ -117,27 +114,27 @@
     groups = blocks // GROUP
     rows = field.shape[0]
     in_smem, in_vmem, in_hbm = (pl.BlockSpec(memory_space=m) for m in (pltpu.SMEM, pltpu.VMEM, pltpu.HBM))
-    far = [pltpu.with_memory_space_constraint(x, pltpu.HBM) for x in (factors, field, before)]
+    far = [pltpu.with_memory_space_constraint(x, pltpu.HBM) for x in (cols, factors, field, before)]
     return pl.pallas_call(
         first_kernel,
         out_shape=[
-            jax.ShapeDtypeStruct((blocks, rows + share, BLOCK), jnp.float32),
+            pltpu.VMEM((blocks, rows + share, BLOCK), jnp.float32),
             pltpu.VMEM((blocks, slots, BLOCK, BLOCK), jnp.bfloat16),
             pltpu.VMEM((share, blocks * BLOCK), jnp.float32),
         ],
-        in_specs=[in_smem, in_smem, in_hbm, in_hbm, in_hbm],
-        out_specs=[pl.BlockSpec(memory_space=pl.ANY), in_vmem, in_vmem],
+        in_specs=[in_smem] + [in_hbm] * 4,
+        out_specs=[in_vmem] * 3,
         scratch_shapes=[
+            pltpu.SMEM(cols.shape, jnp.int32),
             pltpu.VMEM((blocks, BLOCK, 2 * BLOCK), jnp.bfloat16),
             pltpu.VMEM((groups, rows, GROUP * BLOCK), jnp.float32),
             pltpu.VMEM((share, blocks * BLOCK), jnp.float32),
-            pltpu.VMEM((groups, GROUP, rows + share, BLOCK), jnp.float32),
-            pltpu.SemaphoreType.DMA((4, groups)),
+            pltpu.SemaphoreType.DMA((3, groups)),
         ],
         compiler_params=pltpu.CompilerParams(vmem_limit_bytes=VMEM_LIMIT),
         cost_estimate=cost(blocks, slots),
         name="first_right",
-    )(place, cols, *far)
+    )(place, *far)
 
 
 def side(name, read, write, cols, table, field, out):

time: 262 us -> 260 us (level)
  no operation moved by 1% of the time
where the time goes in v7:
time: 260 us
  blocking collectives  242 us (93%)
  Pallas kernels  15.9 us (6%)
    all_to_all x6, blocking collectives, exchange(): return lax.all_to_all(blocks, axis, 0, 0, tiled=True)  242 us
    pallas_call x3, Pallas kernels, side(): pl.pallas_call(functools.partial(later_kernel, read, write), out_shape=pl...  11.1 us

profile of v7, /device:TPU:16, one launch (start us, length us, event | category | flops | bytes accessed | tf_op | source)
XLA Modules:
  0.0 260.0 jit_solution(8024526506984847656)
XLA Ops:
  0.0 4.8 %first_right.1 = (f32[32,144,128]{2,1,0:T(8,128)S(1)}, bf16[32,6,128,128]{3,2,1,0:T(8,128)(2,1)S(1)}, f32[16,4096]{1,0:T(8,128)S(1)}) custom-call(s32[1]{0:T(128)} %bitcast.1.place, s32[6,1,32]{2,1,0:T(1,128)} %bitcast.13, bf16[1,32,6,128,128]{4,3,2,1,0:T(8,128)(2,1)} %factors.1, f32[128,4096]{1,0:T(8,128)} %field.1, f32[128,4096]{1,0:T(8,128)} %before.1), custom_call_target="tpu_custom_call" | custom-call | flops 1610612736 | bytes 10485760 | tf_op jit(solution)/shard_map/first_right/pallas_call | solution.py:118
  4.8 0.0 copy-start
  4.8 68.4 %all_to_all.30.field = f32[32,144,128]{2,1,0:T(8,128)S(1)} all-to-all(f32[32,144,128]{2,1,0:T(8,128)S(1)} %get-tuple-element.9), channel_id=1, replica_groups=mesh['op'=8,'str'=32] {'str'}, dimensions={0} | all-to-all | bytes 4718592 | tf_op jit(solution)/shard_map/all_to_all | solution.py:156
  73.2 0.0 copy-done
  73.2 3.7 %first_left.1 = f32[8,32,16,128]{3,2,1,0:T(8,128)S(1)} custom-call(s32[6,1,32]{2,1,0:T(1,128)S(1)} %bitcast.14, bf16[32,6,128,128]{3,2,1,0:T(8,128)(2,1)S(1)} %get-tuple-element.8.table, f32[32,144,128]{2,1,0:T(8,128)S(1)} %all_to_all.30.field), custom_call_target="tpu_custom_call" | custom-call | flops 1610612736 | bytes 10485760 | tf_op jit(solution)/shard_map/first_left/pallas_call | solution.py:143
  76.9 31.6 %all_to_all.31 = f32[8,32,16,128]{3,2,1,0:T(8,128)S(1)} all-to-all(f32[8,32,16,128]{3,2,1,0:T(8,128)S(1)} %first_left.1), channel_id=1, replica_groups=mesh['op'=8,'str'=32] {'op'}, dimensions={0} | all-to-all | bytes 4194304 | tf_op jit(solution)/shard_map/all_to_all | solution.py:156
  108.5 0.2 slice_subtract_fusion
  108.7 0.2 broadcast_in_dim.4
  108.9 28.6 %all_to_all.32.field = f32[8,32,16,128]{3,2,1,0:T(8,128)S(1)} all-to-all(f32[8,32,16,128]{3,2,1,0:T(8,128)S(1)} %broadcast_in_dim.4), channel_id=1, replica_groups=mesh['op'=8,'str'=32] {'op'}, dimensions={0} | all-to-all | bytes 4194304 | tf_op jit(solution)/shard_map/all_to_all | solution.py:156
  137.5 3.4 %second_left.1 = f32[32,128,128]{2,1,0:T(8,128)S(1)} custom-call(s32[6,1,32]{2,1,0:T(1,128)S(1)} %bitcast.15, bf16[32,6,128,128]{3,2,1,0:T(8,128)(2,1)S(1)} %get-tuple-element.8.table, f32[8,32,16,128]{3,2,1,0:T(8,128)S(1)} %all_to_all.32.field), custom_call_target="tpu_custom_call" | custom-call | flops 1610612736 | bytes 10485760 | tf_op jit(solution)/shard_map/second_left/pallas_call | solution.py:143
  140.8 56.5 %all_to_all.33.field = f32[32,128,128]{2,1,0:T(8,128)S(1)} all-to-all(f32[32,128,128]{2,1,0:T(8,128)S(1)} %second_left.1), channel_id=1, replica_groups=mesh['op'=8,'str'=32] {'str'}, dimensions={0} | all-to-all | bytes 4194304 | tf_op jit(solution)/shard_map/all_to_all | solution.py:156
  197.3 4.0 %second_right.1 = f32[128,4096]{1,0:T(8,128)S(1)} custom-call(s32[6,1,32]{2,1,0:T(1,128)S(1)} %bitcast.16, bf16[32,6,128,128]{3,2,1,0:T(8,128)(2,1)S(1)} %get-tuple-element.8.table, f32[32,128,128]{2,1,0:T(8,128)S(1)} %all_to_all.33.field), custom_call_target="tpu_custom_call" | custom-call | flops 1610612736 | bytes 10485760 | tf_op jit(solution)/shard_map/second_right/pallas_call | solution.py:143
  201.3 29.1 %all_to_all.34 = f32[8,16,4096]{2,1,0:T(8,128)S(1)} all-to-all(f32[8,16,4096]{2,1,0:T(8,128)S(1)} %bitcast.12), channel_id=1, replica_groups=mesh['op'=8,'str'=32] {'op'}, dimensions={0} | all-to-all | bytes 4194304 | tf_op jit(solution)/shard_map/all_to_all | solution.py:156
  230.4 0.1 fusion.2
  230.6 0.2 broadcast_in_dim.5
  230.8 27.9 %all_to_all.35 = f32[8,16,4096]{2,1,0:T(8,128)S(1)} all-to-all(f32[8,16,4096]{2,1,0:T(8,128)S(1)} %broadcast_in_dim.5), channel_id=1, replica_groups=mesh['op'=8,'str'=32] {'op'}, dimensions={0} | all-to-all | bytes 4194304 | tf_op jit(solution)/shard_map/all_to_all | solution.py:156
  258.7 1.3 copy.6
Async XLA Ops:
  4.8 68.4 %copy-start = (s32[1,32,6]{1,0,2:T(1,128)S(1)}, s32[1,32,6]{1,0,2:T(1,128)}, u32[]{:S(2)}) copy-start(s32[1,32,6]{1,0,2:T(1,128)} %param.7) | copy-start | bytes 2308

commit v8 on v7

--- a/solution.py
+++ b/solution.py
@@ -73,13 +73,8 @@
     for c in range(blocks):
         held[c] = jnp.concatenate(halves_of(read(field, c)), axis=1)
 
-    def one(g, carry):
-        for i in range(GROUP):
-            r = g * GROUP + i
-            write(out, r, product(cols, table, held, r))
-        return carry
-
-    lax.fori_loop(0, blocks // GROUP, one, 0)
+    for r in range(blocks):
+        write(out, r, product(cols, table, held, r))
 
 
 def read_turned(field, c):
@@ -101,7 +96,7 @@
 
 
 def write_turned(out, r, total):
-    out[:, pl.ds(pl.multiple_of(r * BLOCK, BLOCK), BLOCK)] = total.T
+    out[:, r * BLOCK : (r + 1) * BLOCK] = total.T
 
 
 def cost(blocks, slots):

time: 260 us -> 258 us (level)
  no operation moved by 1% of the time
where the time goes in v8:
time: 258 us
  blocking collectives  242 us (94%)
  Pallas kernels  14 us (5%)
    all_to_all x6, blocking collectives, exchange(): return lax.all_to_all(blocks, axis, 0, 0, tiled=True)  242 us
    pallas_call x3, Pallas kernels, side(): pl.pallas_call(functools.partial(later_kernel, read, write), out_shape=pl...  9.24 us

profile of v8, /device:TPU:16, one launch (start us, length us, event | category | flops | bytes accessed | tf_op | source)
XLA Modules:
  0.0 258.1 jit_solution(12530119451712350027)
XLA Ops:
  0.0 4.8 %first_right.1 = (f32[32,144,128]{2,1,0:T(8,128)S(1)}, bf16[32,6,128,128]{3,2,1,0:T(8,128)(2,1)S(1)}, f32[16,4096]{1,0:T(8,128)S(1)}) custom-call(s32[1]{0:T(128)} %bitcast.1.place, s32[6,1,32]{2,1,0:T(1,128)} %bitcast.13, bf16[1,32,6,128,128]{4,3,2,1,0:T(8,128)(2,1)} %factors.1, f32[128,4096]{1,0:T(8,128)} %field.1, f32[128,4096]{1,0:T(8,128)} %before.1), custom_call_target="tpu_custom_call" | custom-call | flops 1610612736 | bytes 10485760 | tf_op jit(solution)/shard_map/first_right/pallas_call | solution.py:113
  4.8 0.0 copy-start
  4.8 68.4 %all_to_all.30.field = f32[32,144,128]{2,1,0:T(8,128)S(1)} all-to-all(f32[32,144,128]{2,1,0:T(8,128)S(1)} %get-tuple-element.9), channel_id=1, replica_groups=mesh['op'=8,'str'=32] {'str'}, dimensions={0} | all-to-all | bytes 4718592 | tf_op jit(solution)/shard_map/all_to_all | solution.py:151
  73.2 0.0 copy-done
  73.2 3.2 %first_left.1 = f32[8,32,16,128]{3,2,1,0:T(8,128)S(1)} custom-call(s32[6,1,32]{2,1,0:T(1,128)S(1)} %bitcast.14, bf16[32,6,128,128]{3,2,1,0:T(8,128)(2,1)S(1)} %get-tuple-element.8.table, f32[32,144,128]{2,1,0:T(8,128)S(1)} %all_to_all.30.field), custom_call_target="tpu_custom_call" | custom-call | flops 1610612736 | bytes 10485760 | tf_op jit(solution)/shard_map/first_left/pallas_call | solution.py:138
  76.4 31.6 %all_to_all.31 = f32[8,32,16,128]{3,2,1,0:T(8,128)S(1)} all-to-all(f32[8,32,16,128]{3,2,1,0:T(8,128)S(1)} %first_left.1), channel_id=1, replica_groups=mesh['op'=8,'str'=32] {'op'}, dimensions={0} | all-to-all | bytes 4194304 | tf_op jit(solution)/shard_map/all_to_all | solution.py:151
  108.0 0.2 slice_subtract_fusion
  108.1 0.2 broadcast_in_dim.4
  108.3 28.6 %all_to_all.32.field = f32[8,32,16,128]{3,2,1,0:T(8,128)S(1)} all-to-all(f32[8,32,16,128]{3,2,1,0:T(8,128)S(1)} %broadcast_in_dim.4), channel_id=1, replica_groups=mesh['op'=8,'str'=32] {'op'}, dimensions={0} | all-to-all | bytes 4194304 | tf_op jit(solution)/shard_map/all_to_all | solution.py:151
  136.9 2.9 %second_left.1 = f32[32,128,128]{2,1,0:T(8,128)S(1)} custom-call(s32[6,1,32]{2,1,0:T(1,128)S(1)} %bitcast.15, bf16[32,6,128,128]{3,2,1,0:T(8,128)(2,1)S(1)} %get-tuple-element.8.table, f32[8,32,16,128]{3,2,1,0:T(8,128)S(1)} %all_to_all.32.field), custom_call_target="tpu_custom_call" | custom-call | flops 1610612736 | bytes 10485760 | tf_op jit(solution)/shard_map/second_left/pallas_call | solution.py:138
  139.8 56.5 %all_to_all.33.field = f32[32,128,128]{2,1,0:T(8,128)S(1)} all-to-all(f32[32,128,128]{2,1,0:T(8,128)S(1)} %second_left.1), channel_id=1, replica_groups=mesh['op'=8,'str'=32] {'str'}, dimensions={0} | all-to-all | bytes 4194304 | tf_op jit(solution)/shard_map/all_to_all | solution.py:151
  196.2 3.2 %second_right.1 = f32[128,4096]{1,0:T(8,128)S(1)} custom-call(s32[6,1,32]{2,1,0:T(1,128)S(1)} %bitcast.16, bf16[32,6,128,128]{3,2,1,0:T(8,128)(2,1)S(1)} %get-tuple-element.8.table, f32[32,128,128]{2,1,0:T(8,128)S(1)} %all_to_all.33.field), custom_call_target="tpu_custom_call" | custom-call | flops 1610612736 | bytes 10485760 | tf_op jit(solution)/shard_map/second_right/pallas_call | solution.py:138
  199.5 29.1 %all_to_all.34 = f32[8,16,4096]{2,1,0:T(8,128)S(1)} all-to-all(f32[8,16,4096]{2,1,0:T(8,128)S(1)} %bitcast.12), channel_id=1, replica_groups=mesh['op'=8,'str'=32] {'op'}, dimensions={0} | all-to-all | bytes 4194304 | tf_op jit(solution)/shard_map/all_to_all | solution.py:151
  228.6 0.1 fusion.2
  228.7 0.2 broadcast_in_dim.5
  228.9 27.9 %all_to_all.35 = f32[8,16,4096]{2,1,0:T(8,128)S(1)} all-to-all(f32[8,16,4096]{2,1,0:T(8,128)S(1)} %broadcast_in_dim.5), channel_id=1, replica_groups=mesh['op'=8,'str'=32] {'op'}, dimensions={0} | all-to-all | bytes 4194304 | tf_op jit(solution)/shard_map/all_to_all | solution.py:151
  256.8 1.3 copy.6
Async XLA Ops:
  4.8 68.4 %copy-start = (s32[1,32,6]{1,0,2:T(1,128)S(1)}, s32[1,32,6]{1,0,2:T(1,128)}, u32[]{:S(2)}) copy-start(s32[1,32,6]{1,0,2:T(1,128)} %param.7) | copy-start | bytes 2308
